TPU v7x, 256 devices: a whole 4x4x8 slice. The times are simulated.
256 devices in a mesh: angle: 2 (over y_hi), grid: 2 (over y_lo), slab: 64 (over x, z, core).
Axes of the slice: x: 4, y: 4 (y_hi: 2, y_lo: 2; y = y_hi * 2 + y_lo), z: 8, core: 2. Of those that a mesh axis runs over, the one named last changes fastest.
Arguments:
- efield: float32 [2, 6, 192, 24, 384], P('grid', 'angle', 'slab'), parts along dimension 1, may hold values from -6 to 6
- hfield: float32 [2, 6, 192, 24, 384], P('grid', 'angle', 'slab'), parts along dimension 1, may hold values from -6 to 6
- polar: float32 [2, 6, 192, 24, 384], P('grid', 'angle', 'slab'), parts along dimension 1, may hold values from -3 to 3
- current: float32 [2, 6, 192, 24, 384], P('grid', 'angle', 'slab'), parts along dimension 1, may hold values from -3 to 3
- material: int32 [2, 192, 24, 384], P('grid', 'slab'), may hold values from 0 to 3
- box_offset: int32 [2], replicated, may hold values from 0 to 256, as said below
Outputs:
- efield_final: float32 [2, 6, 192, 24, 384], P('grid', 'angle', 'slab'), parts along dimension 1
- hfield_final: float32 [2, 6, 192, 24, 384], P('grid', 'angle', 'slab'), parts along dimension 1
- polar_final: float32 [2, 6, 192, 24, 384], P('grid', 'angle', 'slab'), parts along dimension 1
- current_final: float32 [2, 6, 192, 24, 384], P('grid', 'angle', 'slab'), parts along dimension 1
There are 2 independent parts, one for each index of `angle`. A program takes and returns all parts, laid end to end along the dimension named above; an argument that names none is the same for every part. Nothing has to cross between parts.
Inputs may be any that keep to these rules, and one draw needn't show every extreme that they name: `box_offset`: entry 0 lies in 0 to 16; entry 1 is 256, so that the box lies inside the coarse grid and reaches its last z cells.
All inputs are finite; a program needn't handle non-finite values.
Results may differ from a plain program's by a relative error of at most 0.0001.
Values sent between devices are 32-bit elements; how exact they have to be, the bound alone decides.
A program may use at most 64 MiB of HBM per device.

v0:
```python
import jax
import jax.numpy as jnp
from jax import lax
from jax.sharding import PartitionSpec as P

STEPS = 3


PERMITTIVITY = (1.0, 1.5, 1.2, 2.0)
STRENGTH = (0.4, 0.9, 0.3, 1.1)
RESONANCE = (0.6, 0.5, 0.8, 0.3)
DAMPING_RATE = (0.3, 0.2, 0.05, 0.4)
COURANT = 0.5
STEP_COARSE = 0.5
STEP_FINE = STEP_COARSE / 3.0


def shifted(value, axis, steps):
    count = lax.axis_size(axis)
    first, last = (max(0, -steps), min(count, count - steps))
    return lax.ppermute(value, axis, [(source, source + steps) for source in range(first, last)])


def lookup(material, values_table):
    values = jnp.zeros(material.shape, jnp.float32)
    for material_id in range(4):
        values = values + jnp.where(
            material == material_id, jnp.float32(values_table[material_id]), jnp.float32(0.0)
        )
    return values


def coefficients(material):
    return (
        lookup(material, PERMITTIVITY),
        lookup(material, STRENGTH),
        lookup(material, RESONANCE),
        lookup(material, DAMPING_RATE),
    )


def shifted_down(field, dimension):
    widths = [(0, 0)] * field.ndim
    widths[dimension] = (1, 0)
    return lax.slice_in_dim(jnp.pad(field, widths), 0, field.shape[dimension], axis=dimension)


def shifted_up(field, dimension):
    widths = [(0, 0)] * field.ndim
    widths[dimension] = (0, 1)
    return lax.slice_in_dim(jnp.pad(field, widths), 1, field.shape[dimension] + 1, axis=dimension)


def advance(fields, material_terms, curl_scale, step_size):
    efield, hfield, polar, current = fields
    permittivity, strength, resonance, damping = material_terms
    hfield_x, hfield_y, hfield_z = (hfield[0], hfield[1], hfield[2])
    below_plane = shifted(hfield[1:3, -1:], "slab", 1)
    hfield_y_back = jnp.concatenate([below_plane[0], hfield_y[:-1]], axis=0)
    hfield_z_back = jnp.concatenate([below_plane[1], hfield_z[:-1]], axis=0)
    curl_h = jnp.stack(
        [
            hfield_z - shifted_down(hfield_z, 1) - (hfield_y - shifted_down(hfield_y, 2)),
            hfield_x - shifted_down(hfield_x, 2) - (hfield_z - hfield_z_back),
            hfield_y - hfield_y_back - (hfield_x - shifted_down(hfield_x, 1)),
        ]
    )
    current = current + step_size * (
        -damping * current - resonance * polar + strength * resonance * efield
    )
    polar = polar + step_size * current
    efield = efield + (curl_scale * curl_h - step_size * current) / permittivity
    efield_x, efield_y, efield_z = (efield[0], efield[1], efield[2])
    above_plane = shifted(efield[1:3, :1], "slab", -1)
    efield_y_next = jnp.concatenate([efield_y[1:], above_plane[0]], axis=0)
    efield_z_next = jnp.concatenate([efield_z[1:], above_plane[1]], axis=0)
    curl_e = jnp.stack(
        [
            shifted_up(efield_z, 1) - efield_z - (shifted_up(efield_y, 2) - efield_y),
            shifted_up(efield_x, 2) - efield_x - (efield_z_next - efield_z),
            efield_y_next - efield_y - (shifted_up(efield_x, 1) - efield_x),
        ]
    )
    hfield = hfield - curl_scale * curl_e
    return (efield, hfield, polar, current)


def upsample(section):
    components, length_x, length_y, length_z = section.shape
    expanded = jnp.broadcast_to(
        section[:, :, None, :, None, :, None], (components, length_x, 3, length_y, 3, length_z, 3)
    )
    return expanded.reshape(components, 3 * length_x, 3 * length_y, 3 * length_z)


def restrict(field):
    components, length_x, length_y, length_z = field.shape
    return jnp.mean(
        field.reshape(components, length_x // 3, 3, length_y // 3, 3, length_z // 3, 3),
        axis=(2, 4, 6),
    )


def on_device(efield, hfield, polar, current, material, box_offset):
    level_index = lax.axis_index("grid")
    slab_index = lax.axis_index("slab")
    slab_count = lax.axis_size("slab")
    planes = efield.shape[2]
    width_y = efield.shape[3]
    depth_z = efield.shape[4]
    plane_fine = planes // 3
    box_y = width_y // 3
    box_z = depth_z // 3
    first_slab = slab_count // 8
    start_x = first_slab * planes
    box_x = slab_count * plane_fine
    is_fine = level_index == 1
    anchor = jnp.int32(0)
    corner_y = box_offset[0]
    corner_z = box_offset[1]
    material_terms = coefficients(material[0])
    fields = (efield[0], hfield[0], polar[0], current[0])
    global_x = slab_index * planes + jnp.arange(planes, dtype=jnp.int32)
    position_x = global_x[:, None, None]
    position_y = jnp.arange(width_y, dtype=jnp.int32)[None, :, None]
    position_z = jnp.arange(depth_z, dtype=jnp.int32)[None, None, :]
    rim_cells = is_fine & (
        (position_x == 0)
        | (position_x == slab_count * planes - 1)
        | (position_y == 0)
        | (position_y == width_y - 1)
        | (position_z == 0)
        | (position_z == depth_z - 1)
    )
    inside = (
        (level_index == 0)
        & (position_x >= start_x + 1)
        & (position_x <= start_x + box_x - 2)
        & (position_y >= corner_y + 1)
        & (position_y <= corner_y + box_y - 2)
        & (position_z >= corner_z + 1)
        & (position_z <= corner_z + box_z - 2)
    )

    def inject(field):
        section = lax.dynamic_slice(
            field, (anchor, anchor, corner_y, corner_z), (3, planes, box_y, box_z)
        )
        whole_grid = lax.all_gather(section, "slab", axis=1, tiled=True)
        own_planes = lax.dynamic_slice_in_dim(
            whole_grid, start_x + slab_index * plane_fine, plane_fine, 1
        )
        return shifted(own_planes, "grid", 1)

    previous = inject(fields[0])
    latest = previous
    for step_index in range(STEPS):
        for sub_index in range(3):
            if sub_index == 0:
                curl_scale = jnp.float32(COURANT)
                step_size = jnp.where(is_fine, jnp.float32(STEP_FINE), jnp.float32(STEP_COARSE))
            else:
                curl_scale = jnp.where(is_fine, jnp.float32(COURANT), jnp.float32(0.0))
                step_size = jnp.where(is_fine, jnp.float32(STEP_FINE), jnp.float32(0.0))
            fields = advance(fields, material_terms, curl_scale, step_size)
            if sub_index == 0:
                latest = inject(fields[0])
            weight = (sub_index + 1) / 3.0
            boundary = upsample(previous + weight * (latest - previous))
            fields = (jnp.where(rim_cells, boundary, fields[0]),) + fields[1:]
        previous = latest
        feedback_field = fields[0]
        averaged = restrict(feedback_field)
        arrived = shifted(averaged, "grid", -1)
        box_strip = lax.all_gather(arrived, "slab", axis=1, tiled=True)
        box_strip = jnp.pad(box_strip, ((0, 0), (0, planes), (0, 0), (0, 0)))
        box_block = lax.dynamic_slice_in_dim(box_strip, slab_index * planes - start_x, planes, 1)
        placed = lax.dynamic_update_slice(
            jnp.zeros_like(feedback_field), box_block, (anchor, anchor, corner_y, corner_z)
        )
        fields = (jnp.where(inside, placed, feedback_field),) + fields[1:]
    return (fields[0][None], fields[1][None], fields[2][None], fields[3][None])


def solution(mesh):
    return jax.shard_map(
        on_device,
        mesh=mesh,
        in_specs=(
            P("grid", "angle", "slab", None, None),
            P("grid", "angle", "slab", None, None),
            P("grid", "angle", "slab", None, None),
            P("grid", "angle", "slab", None, None),
            P("grid", "slab", None, None),
            P(),
        ),
        out_specs=(
            P("grid", "angle", "slab", None, None),
            P("grid", "angle", "slab", None, None),
            P("grid", "angle", "slab", None, None),
            P("grid", "angle", "slab", None, None),
        ),
        check_vma=False,
    )
```

profile of v0, /device:TPU:99, one launch (start us, length us, event | category | flops | bytes accessed | tf_op | source)
XLA Modules:
  0.0 687.0 jit_solution(6722522991202542338)
XLA Ops:
  15.0 5.3 collective-permute-start.1
  29.9 1.9 collective-permute-start.3
  32.0 5.0 collective-permute-done.3
  37.2 1.9 collective-permute-start.4
  40.5 52.0 %all-gather.12.cloned.1.call-done = f32[1,3,192,8,128]{4,3,2,1,0:T(8,128)} async-done(((f32[1,3,3,8,128]{4,3,2,1,0:T(8,128)}), f32[1,3,192,8,128]{4,3,2,1,0:T(8,128)}) %all-gather.12.cloned.1.call-update) | async-done | bytes 2359312 | tf_op jit(solution)/shard_map/all_gather | solution.py:149
  93.2 3.1 collective-permute-start
  96.3 74.6 %all-gather.6.cloned.1.call-done = f32[3,192,8,128]{3,2,1,0:T(8,128)} async-done(((f32[3,3,8,128]{3,2,1,0:T(8,128)}), f32[3,192,8,128]{3,2,1,0:T(8,128)}) %all-gather.6.cloned.1.call-update) | async-done | bytes 2359312 | tf_op jit(solution)/shard_map/all_gather | solution.py:149
  171.6 3.1 collective-permute-start.2
  175.6 2.8 broadcast_in_dim.270
  178.4 3.8 broadcast_in_dim.271
  182.5 3.0 collective-permute-start.5
  185.6 2.8 broadcast_in_dim.262
  188.4 3.8 broadcast_in_dim.263
  192.3 2.8 broadcast_in_dim.266
  195.1 4.4 broadcast_in_dim.267
  200.0 3.8 collective-permute-start.6
  207.7 2.9 collective-permute-start.8
  211.2 6.9 %reduce_sum.37 = f32[3,8,3,128,3]{4,3,2,1,0:T(8,128)} reshape(f32[3,24,384]{2,1,0:T(8,128)S(1)} %fusion.60) | data formatting | bytes 221184 | tf_op jit(solution)/shard_map/reduce_sum | solution.py:98
  218.1 2.8 reduce_sum.38
  223.0 2.3 collective-permute-done.7
  225.4 51.6 %all_gather.23 = f32[3,64,8,128]{3,2,0,1:T(8,128)S(1)} all-gather(f32[3,1,8,128]{3,2,0,1:T(8,128)S(1)} %collective-permute-done.7), channel_id=1, replica_groups=mesh['angle'=2,'grid'=2,'slab'=64] {'slab'}, dimensions={1}, use_global_device_ids=true | all-gather | bytes 798720 | tf_op jit(solution)/shard_map/all_gather | solution.py:175
  279.8 3.2 collective-permute-start.9
  284.6 2.4 fusion.26
  287.7 3.1 collective-permute-start.11
  291.0 4.2 collective-permute-done.11
  295.5 1.9 collective-permute-start.12
  298.8 66.6 %all-gather.8.cloned.1.call-done = f32[3,192,8,128]{3,2,1,0:T(8,128)} async-done(((f32[3,3,8,128]{3,2,1,0:T(8,128)}), f32[3,192,8,128]{3,2,1,0:T(8,128)}) %all-gather.8.cloned.1.call-update) | async-done | bytes 2359312 | tf_op jit(solution)/shard_map/all_gather | solution.py:149
  366.1 3.1 collective-permute-start.10
  370.0 2.8 broadcast_in_dim.285
  372.9 4.4 broadcast_in_dim.286
  377.3 2.1 fusion.30
  379.4 3.2 collective-permute-start.13
  382.7 2.8 broadcast_in_dim.281
  385.5 4.4 broadcast_in_dim.282
  389.9 2.8 broadcast_in_dim.277
  392.7 3.8 broadcast_in_dim.278
  396.9 3.8 collective-permute-start.14
  405.3 2.4 collective-permute-start.16
  407.7 6.3 reduce_sum.40
  414.0 2.8 reduce_sum.44
  419.0 2.3 collective-permute-done.15
  421.3 51.6 %all_gather.25 = f32[3,64,8,128]{3,2,0,1:T(8,128)S(1)} all-gather(f32[3,1,8,128]{3,2,0,1:T(8,128)S(1)} %collective-permute-done.15), channel_id=1, replica_groups=mesh['angle'=2,'grid'=2,'slab'=64] {'slab'}, dimensions={1}, use_global_device_ids=true | all-gather | bytes 798720 | tf_op jit(solution)/shard_map/all_gather | solution.py:175
  475.9 3.2 collective-permute-start.17
  480.6 2.2 fusion.38
  494.3 3.1 collective-permute-start.19
  498.4 4.0 collective-permute-done.19
  503.4 1.9 collective-permute-start.20
  508.0 53.3 %all-gather.10.cloned.1.call-done = f32[3,192,8,128]{3,2,1,0:T(8,128)} async-done(((f32[3,3,8,128]{3,2,1,0:T(8,128)}), f32[3,192,8,128]{3,2,1,0:T(8,128)}) %all-gather.10.cloned.1.call-update) | async-done | bytes 2359312 | tf_op jit(solution)/shard_map/all_gather | solution.py:149
  562.0 3.3 collective-permute-start.18
  565.3 1.9 fusion.177
  567.2 2.8 broadcast_in_dim.293
  570.0 4.4 broadcast_in_dim.294
  574.4 2.8 broadcast_in_dim.297
  577.2 4.4 broadcast_in_dim.298
  582.9 2.2 add_bitcast_fusion
  586.6 2.4 collective-permute-start.21
  589.1 2.8 broadcast_in_dim.289
  591.9 4.4 broadcast_in_dim.290
  598.7 4.3 collective-permute-start.22
  606.0 1.9 collective-permute-start.24
  607.9 6.9 %reduce_sum.55 = f32[3,8,3,128,3]{4,3,2,1,0:T(8,128)} reshape(f32[3,24,384]{2,1,0:T(8,128)S(1)} %get-tuple-element.7) | data formatting | bytes 221184 | tf_op jit(solution)/shard_map/reduce_sum | solution.py:98
  614.8 2.9 reduce_sum.56
  622.2 52.3 %all_gather.27 = f32[3,64,8,128]{3,2,0,1:T(8,128)S(1)} all-gather(f32[3,1,8,128]{3,2,0,1:T(8,128)S(1)} %collective-permute-done.23), channel_id=1, replica_groups=mesh['angle'=2,'grid'=2,'slab'=64] {'slab'}, dimensions={1}, use_global_device_ids=true | all-gather | bytes 798720 | tf_op jit(solution)/shard_map/all_gather | solution.py:175
  678.0 2.1 fusion.55
  (320 shorter events, 74.5 us)
Async XLA Ops:
  7.2 29.9 %copy-start = (f32[1,3,3,24,384]{4,3,2,1,0:T(8,128)S(1)}, f32[1,3,3,24,384]{4,3,2,1,0:T(8,128)}, u32[]{:S(2)}) copy-start(f32[1,3,3,24,384]{4,3,2,1,0:T(8,128)} %param.7) | copy-start | bytes 995332
  7.2 85.3 %all-gather.12.cloned.1.call-start = ((), (), s32[]{:S(2)}) async-start(), calls=%async_computation.3 | async-start | bytes 2396160 | tf_op jit(solution)/shard_map/all_gather | solution.py:149
  14.0 156.9 %all-gather.6.cloned.1.call-start = ((), (), s32[]{:S(2)}) async-start(), calls=%async_computation | async-start | bytes 2396160 | tf_op jit(solution)/shard_map/all_gather | solution.py:149
  15.0 8.4 %collective-permute-start.1 = (f32[2,1,24,384]{3,2,1,0:T(8,128)S(1)}, f32[2,1,24,384]{3,2,1,0:T(8,128)S(1)}, u32[]{:S(2)}, u32[]{:S(2)}) collective-permute-start(f32[2,1,24,384]{3,2,1,0:T(8,128)S(1)} %slice.1055), channel_id=1, source_target_pairs={{0,1},{1,2},{2,3},{3,4},{4,5},{5,6},{6,7},{7,8},{8,9},{9,10},{10,1... | collective-permute-start | bytes 221192 | tf_op jit(solution)/shard_map/ppermute | solution.py:21
  24.5 12.6 %copy-start.50 = (f32[3,24,384]{2,1,0:T(8,128)}, f32[3,24,384]{2,1,0:T(8,128)S(1)}, u32[]{:S(2)}) copy-start(f32[3,24,384]{2,1,0:T(8,128)S(1)} %get-tuple-element.207) | copy-start | bytes 331780
  26.7 338.7 %all-gather.8.cloned.1.call-start = ((), (), s32[]{:S(2)}) async-start(), calls=%async_computation.1 | async-start | bytes 2396160 | tf_op jit(solution)/shard_map/all_gather | solution.py:149
  29.9 7.1 %collective-permute-start.3 = (f32[2,1,24,384]{3,2,1,0:T(8,128)S(1)}, f32[2,1,24,384]{3,2,1,0:T(8,128)S(1)}, u32[]{:S(2)}, u32[]{:S(2)}) collective-permute-start(f32[2,1,24,384]{3,2,1,0:T(8,128)S(1)} %slice.1062), channel_id=1, source_target_pairs={{1,0},{2,1},{3,2},{4,3},{5,4},{6,5},{7,6},{8,7},{9,8},{10,9},{11,1... | collective-permute-start | bytes 221192 | tf_op jit(solution)/shard_map/ppermute | solution.py:21
  37.2 3.3 collective-permute-start.4
  93.2 81.7 %collective-permute-start = (f32[3,1,8,128]{3,2,1,0:T(8,128)S(1)}, f32[3,1,8,128]{3,2,1,0:T(8,128)S(1)}, u32[]{:S(2)}, u32[]{:S(2)}) collective-permute-start(f32[3,1,8,128]{3,2,1,0:T(8,128)S(1)} %dynamic-slice_bitcast_fusion), channel_id=1, source_target_pairs={{0,64},{1,65},{2,66},{3,67},{4,68},{5,69},{6,70},{7,71},{8,72},{9,... | collective-permute-start | bytes 36872 | tf_op jit(solution)/shard_map/ppermute | solution.py:21
  171.6 3.9 collective-permute-start.2
  182.2 28.4 %copy-start.6 = (f32[3,24,384]{2,1,0:T(8,128)}, f32[3,24,384]{2,1,0:T(8,128)S(1)}, u32[]{:S(2)}) copy-start(f32[3,24,384]{2,1,0:T(8,128)S(1)} %broadcast_in_dim.271) | copy-start | bytes 331780
  182.5 9.8 %copy-start.29 = (f32[3,24,384]{2,1,0:T(8,128)}, f32[3,24,384]{2,1,0:T(8,128)S(1)}, u32[]{:S(2)}) copy-start(f32[3,24,384]{2,1,0:T(8,128)S(1)} %get-tuple-element.137) | copy-start | bytes 331780
  182.5 9.8 %copy-start.30 = (f32[3,24,384]{2,1,0:T(8,128)}, f32[3,24,384]{2,1,0:T(8,128)S(1)}, u32[]{:S(2)}) copy-start(f32[3,24,384]{2,1,0:T(8,128)S(1)} %get-tuple-element.139) | copy-start | bytes 331780
  182.5 17.1 %collective-permute-start.5 = (f32[2,1,24,384]{3,2,1,0:T(8,128)S(1)}, f32[2,1,24,384]{3,2,1,0:T(8,128)S(1)}, u32[]{:S(2)}, u32[]{:S(2)}) collective-permute-start(f32[2,1,24,384]{3,2,1,0:T(8,128)S(1)} %slice.1078), channel_id=1, source_target_pairs={{1,0},{2,1},{3,2},{4,3},{5,4},{6,5},{7,6},{8,7},{9,8},{10,9},{11,1... | collective-permute-start | bytes 221192 | tf_op jit(solution)/shard_map/ppermute | solution.py:21
  192.2 18.4 %copy-start.23 = (f32[3,24,384]{2,1,0:T(8,128)}, f32[3,24,384]{2,1,0:T(8,128)S(1)}, u32[]{:S(2)}) copy-start(f32[3,24,384]{2,1,0:T(8,128)S(1)} %broadcast_in_dim.263) | copy-start | bytes 331780
  199.5 11.2 %copy-start.13 = (f32[1,3,3,24,384]{4,3,2,1,0:T(8,128)S(1)}, f32[1,3,3,24,384]{4,3,2,1,0:T(8,128)}, u32[]{:S(2)}) copy-start(f32[1,3,3,24,384]{4,3,2,1,0:T(8,128)} %param.6) | copy-start | bytes 995332
  199.5 11.2 %copy-start.17 = (f32[1,3,3,24,384]{4,3,2,1,0:T(8,128)S(1)}, f32[1,3,3,24,384]{4,3,2,1,0:T(8,128)}, u32[]{:S(2)}) copy-start(f32[1,3,3,24,384]{4,3,2,1,0:T(8,128)} %param.9) | copy-start | bytes 995332
  199.5 11.2 %copy-start.38 = (f32[3,24,384]{2,1,0:T(8,128)S(1)}, f32[3,24,384]{2,1,0:T(8,128)}, u32[]{:S(2)}) copy-start(f32[3,24,384]{2,1,0:T(8,128)} %copy-done.37) | copy-start | bytes 331780
  199.5 11.2 %copy-start.40 = (f32[3,24,384]{2,1,0:T(8,128)S(1)}, f32[3,24,384]{2,1,0:T(8,128)}, u32[]{:S(2)}) copy-start(f32[3,24,384]{2,1,0:T(8,128)} %copy-done.39) | copy-start | bytes 331780
  199.5 11.2 %copy-start.47 = (f32[3,24,384]{2,1,0:T(8,128)S(1)}, f32[3,24,384]{2,1,0:T(8,128)}, u32[]{:S(2)}) copy-start(f32[3,24,384]{2,1,0:T(8,128)} %copy-done.46) | copy-start | bytes 331780
  199.5 11.2 %copy-start.49 = (f32[3,24,384]{2,1,0:T(8,128)S(1)}, f32[3,24,384]{2,1,0:T(8,128)}, u32[]{:S(2)}) copy-start(f32[3,24,384]{2,1,0:T(8,128)} %copy-done.48) | copy-start | bytes 331780
  199.5 11.2 %copy-start.51 = (f32[3,24,384]{2,1,0:T(8,128)S(1)}, f32[3,24,384]{2,1,0:T(8,128)}, u32[]{:S(2)}) copy-start(f32[3,24,384]{2,1,0:T(8,128)} %copy-done.50) | copy-start | bytes 331780
  199.5 11.2 %copy-start.57 = (f32[1,1,3,24,384]{4,3,2,1,0:T(8,128)S(1)}, f32[1,1,3,24,384]{4,3,2,1,0:T(8,128)}, u32[]{:S(2)}) copy-start(f32[1,1,3,24,384]{4,3,2,1,0:T(8,128)} %fusion.227) | copy-start | bytes 331780
  200.0 5.2 collective-permute-start.6
  207.6 14.6 %copy-start.31 = (f32[3,24,384]{2,1,0:T(8,128)}, f32[3,24,384]{2,1,0:T(8,128)S(1)}, u32[]{:S(2)}) copy-start(f32[3,24,384]{2,1,0:T(8,128)S(1)} %get-tuple-element.127) | copy-start | bytes 331780
  207.6 14.6 %copy-start.32 = (f32[3,24,384]{2,1,0:T(8,128)}, f32[3,24,384]{2,1,0:T(8,128)S(1)}, u32[]{:S(2)}) copy-start(f32[3,24,384]{2,1,0:T(8,128)S(1)} %get-tuple-element.129) | copy-start | bytes 331780
  207.7 70.0 %collective-permute-start.8 = (f32[2,1,24,384]{3,2,1,0:T(8,128)}, f32[2,1,24,384]{3,2,1,0:T(8,128)}, u32[]{:S(2)}, u32[]{:S(2)}) collective-permute-start(f32[2,1,24,384]{3,2,1,0:T(8,128)} %slice.1094), channel_id=1, source_target_pairs={{1,0},{2,1},{3,2},{4,3},{5,4},{6,5},{7,6},{8,7},{9,8},{10,9},{11,1... | collective-permute-start | bytes 221192 | tf_op jit(solution)/shard_map/ppermute | solution.py:21
  220.9 4.4 collective-permute-start.7
  279.8 4.6 collective-permute-start.9
  287.6 273.6 %all-gather.10.cloned.1.call-start = ((), (), s32[]{:S(2)}) async-start(), calls=%async_computation.2 | async-start | bytes 2396160 | tf_op jit(solution)/shard_map/all_gather | solution.py:149
  287.7 7.5 %collective-permute-start.11 = (f32[2,1,24,384]{3,2,1,0:T(8,128)S(1)}, f32[2,1,24,384]{3,2,1,0:T(8,128)S(1)}, u32[]{:S(2)}, u32[]{:S(2)}) collective-permute-start(f32[2,1,24,384]{3,2,1,0:T(8,128)S(1)} %slice.1110), channel_id=1, source_target_pairs={{1,0},{2,1},{3,2},{4,3},{5,4},{6,5},{7,6},{8,7},{9,8},{10,9},{11,1... | collective-permute-start | bytes 221192 | tf_op jit(solution)/shard_map/ppermute | solution.py:21
  290.9 82.0 %copy-start.33 = (f32[3,24,384]{2,1,0:T(8,128)}, f32[3,24,384]{2,1,0:T(8,128)S(1)}, u32[]{:S(2)}) copy-start(f32[3,24,384]{2,1,0:T(8,128)S(1)} %get-tuple-element.117) | copy-start | bytes 331780
  290.9 82.0 %copy-start.34 = (f32[3,24,384]{2,1,0:T(8,128)}, f32[3,24,384]{2,1,0:T(8,128)S(1)}, u32[]{:S(2)}) copy-start(f32[3,24,384]{2,1,0:T(8,128)S(1)} %get-tuple-element.119) | copy-start | bytes 331780
  295.5 3.3 collective-permute-start.12
  366.1 3.9 collective-permute-start.10
  379.4 10.6 %copy-start.35 = (f32[3,24,384]{2,1,0:T(8,128)}, f32[3,24,384]{2,1,0:T(8,128)S(1)}, u32[]{:S(2)}) copy-start(f32[3,24,384]{2,1,0:T(8,128)S(1)} %get-tuple-element.107) | copy-start | bytes 331780
  379.4 10.6 %copy-start.36 = (f32[3,24,384]{2,1,0:T(8,128)}, f32[3,24,384]{2,1,0:T(8,128)S(1)}, u32[]{:S(2)}) copy-start(f32[3,24,384]{2,1,0:T(8,128)S(1)} %get-tuple-element.109) | copy-start | bytes 331780
  379.4 17.2 %collective-permute-start.13 = (f32[2,1,24,384]{3,2,1,0:T(8,128)S(1)}, f32[2,1,24,384]{3,2,1,0:T(8,128)S(1)}, u32[]{:S(2)}, u32[]{:S(2)}) collective-permute-start(f32[2,1,24,384]{3,2,1,0:T(8,128)S(1)} %slice.1126), channel_id=1, source_target_pairs={{1,0},{2,1},{3,2},{4,3},{5,4},{6,5},{7,6},{8,7},{9,8},{10,9},{11,1... | collective-permute-start | bytes 221192 | tf_op jit(solution)/shard_map/ppermute | solution.py:21
  396.5 8.7 %copy-start.44 = (f32[3,24,384]{2,1,0:T(8,128)}, f32[3,24,384]{2,1,0:T(8,128)S(1)}, u32[]{:S(2)}) copy-start(f32[3,24,384]{2,1,0:T(8,128)S(1)} %broadcast_in_dim.278) | copy-start | bytes 331780
  396.9 5.1 collective-permute-start.14
  405.3 12.9 %copy-start.41 = (f32[3,24,384]{2,1,0:T(8,128)}, f32[3,24,384]{2,1,0:T(8,128)S(1)}, u32[]{:S(2)}) copy-start(f32[3,24,384]{2,1,0:T(8,128)S(1)} %get-tuple-element.97) | copy-start | bytes 331780
  405.3 12.9 %copy-start.42 = (f32[3,24,384]{2,1,0:T(8,128)}, f32[3,24,384]{2,1,0:T(8,128)S(1)}, u32[]{:S(2)}) copy-start(f32[3,24,384]{2,1,0:T(8,128)S(1)} %get-tuple-element.99) | copy-start | bytes 331780
  405.3 68.2 %collective-permute-start.16 = (f32[2,1,24,384]{3,2,1,0:T(8,128)}, f32[2,1,24,384]{3,2,1,0:T(8,128)}, u32[]{:S(2)}, u32[]{:S(2)}) collective-permute-start(f32[2,1,24,384]{3,2,1,0:T(8,128)} %slice.1142), channel_id=1, source_target_pairs={{1,0},{2,1},{3,2},{4,3},{5,4},{6,5},{7,6},{8,7},{9,8},{10,9},{11,1... | collective-permute-start | bytes 221192 | tf_op jit(solution)/shard_map/ppermute | solution.py:21
  416.9 4.4 collective-permute-start.15
  418.3 64.5 %copy-start.10 = (f32[1,3,24,384]{3,2,1,0:T(8,128)}, f32[1,3,24,384]{3,2,1,0:T(8,128)S(1)}, u32[]{:S(2)}) copy-start(f32[1,3,24,384]{3,2,1,0:T(8,128)S(1)} %fusion.224) | copy-start | bytes 331780
  475.9 4.6 collective-permute-start.17
  483.5 19.7 %copy-start.11 = (f32[1,3,24,384]{3,2,1,0:T(8,128)S(1)}, f32[1,3,24,384]{3,2,1,0:T(8,128)}, u32[]{:S(2)}) copy-start(f32[1,3,24,384]{3,2,1,0:T(8,128)} %copy-done.10) | copy-start | bytes 331780
  494.3 8.0 %collective-permute-start.19 = (f32[2,1,24,384]{3,2,1,0:T(8,128)S(1)}, f32[2,1,24,384]{3,2,1,0:T(8,128)S(1)}, u32[]{:S(2)}, u32[]{:S(2)}) collective-permute-start(f32[2,1,24,384]{3,2,1,0:T(8,128)S(1)} %slice.1158), channel_id=1, source_target_pairs={{1,0},{2,1},{3,2},{4,3},{5,4},{6,5},{7,6},{8,7},{9,8},{10,9},{11,1... | collective-permute-start | bytes 221192 | tf_op jit(solution)/shard_map/ppermute | solution.py:21
  503.4 4.0 collective-permute-start.20
  562.0 5.2 collective-permute-start.18
  586.6 9.7 %collective-permute-start.21 = (f32[2,1,24,384]{3,2,1,0:T(8,128)S(1)}, f32[2,1,24,384]{3,2,1,0:T(8,128)}, u32[]{:S(2)}, u32[]{:S(2)}) collective-permute-start(f32[2,1,24,384]{3,2,1,0:T(8,128)S(1)} %slice.1174), channel_id=1, source_target_pairs={{1,0},{2,1},{3,2},{4,3},{5,4},{6,5},{7,6},{8,7},{9,8},{10,9},{11,1... | collective-permute-start | bytes 221192 | tf_op jit(solution)/shard_map/ppermute | solution.py:21
  589.1 8.2 %copy-start.8 = (f32[3,24,384]{2,1,0:T(8,128)S(1)}, f32[3,24,384]{2,1,0:T(8,128)}, u32[]{:S(2)}) copy-start(f32[3,24,384]{2,1,0:T(8,128)} %copy-done.7) | copy-start | bytes 331780
  589.1 8.2 %copy-start.12 = (f32[1,3,24,384]{3,2,1,0:T(8,128)S(1)}, f32[1,3,24,384]{3,2,1,0:T(8,128)}, u32[]{:S(2)}) copy-start(f32[1,3,24,384]{3,2,1,0:T(8,128)} %copy-done.10) | copy-start | bytes 331780
  598.7 5.7 collective-permute-start.22
  606.0 70.0 %collective-permute-start.24 = (f32[2,1,24,384]{3,2,1,0:T(8,128)}, f32[2,1,24,384]{3,2,1,0:T(8,128)}, u32[]{:S(2)}, u32[]{:S(2)}) collective-permute-start(f32[2,1,24,384]{3,2,1,0:T(8,128)} %slice.1190), channel_id=1, source_target_pairs={{1,0},{2,1},{3,2},{4,3},{5,4},{6,5},{7,6},{8,7},{9,8},{10,9},{11,1... | collective-permute-start | bytes 221192 | tf_op jit(solution)/shard_map/ppermute | solution.py:21
  614.8 60.4 %copy-start.25 = (f32[3,24,384]{2,1,0:T(8,128)S(1)}, f32[3,24,384]{2,1,0:T(8,128)}, u32[]{:S(2)}) copy-start(f32[3,24,384]{2,1,0:T(8,128)} %broadcast_in_dim.290) | copy-start | bytes 331780
  614.8 63.2 %copy-start.9 = (f32[3,24,384]{2,1,0:T(8,128)S(1)}, f32[3,24,384]{2,1,0:T(8,128)}, u32[]{:S(2)}) copy-start(f32[3,24,384]{2,1,0:T(8,128)} %copy-done.7) | copy-start | bytes 331780
  614.8 63.2 %copy-start.20 = (f32[3,24,384]{2,1,0:T(8,128)S(1)}, f32[3,24,384]{2,1,0:T(8,128)}, u32[]{:S(2)}) copy-start(f32[3,24,384]{2,1,0:T(8,128)} %copy-done.19) | copy-start | bytes 331780
  614.8 63.2 %copy-start.22 = (f32[3,24,384]{2,1,0:T(8,128)S(1)}, f32[3,24,384]{2,1,0:T(8,128)}, u32[]{:S(2)}) copy-start(f32[3,24,384]{2,1,0:T(8,128)} %copy-done.21) | copy-start | bytes 331780
  614.8 63.2 %copy-start.52 = (f32[1,1,3,24,384]{4,3,2,1,0:T(8,128)S(1)}, f32[1,1,3,24,384]{4,3,2,1,0:T(8,128)}, u32[]{:S(2)}) copy-start(f32[1,1,3,24,384]{4,3,2,1,0:T(8,128)} %fusion.221) | copy-start | bytes 331780
  614.8 63.2 %copy-start.53 = (f32[1,1,3,24,384]{4,3,2,1,0:T(8,128)S(1)}, f32[1,1,3,24,384]{4,3,2,1,0:T(8,128)}, u32[]{:S(2)}) copy-start(f32[1,1,3,24,384]{4,3,2,1,0:T(8,128)} %fusion.220) | copy-start | bytes 331780
  614.8 63.2 %copy-start.54 = (f32[1,1,3,24,384]{4,3,2,1,0:T(8,128)S(1)}, f32[1,1,3,24,384]{4,3,2,1,0:T(8,128)}, u32[]{:S(2)}) copy-start(f32[1,1,3,24,384]{4,3,2,1,0:T(8,128)} %fusion.219) | copy-start | bytes 331780
  614.8 63.2 %copy-start.55 = (f32[1,1,3,24,384]{4,3,2,1,0:T(8,128)S(1)}, f32[1,1,3,24,384]{4,3,2,1,0:T(8,128)}, u32[]{:S(2)}) copy-start(f32[1,1,3,24,384]{4,3,2,1,0:T(8,128)} %fusion.218) | copy-start | bytes 331780
  617.8 4.4 collective-permute-start.23
  (24 other events, 147.1 us)
Sparse Core Ops, SparseCore 0:
  14.2 78.2 all-gather.11
  95.7 75.1 all-gather.5
  287.8 77.5 all-gather.7
  483.6 77.5 all-gather.9
where the time goes:
time: 700 us; the launch traced here: 687 us
  waiting for transfers between devices  274 us (39%)
  blocking collectives  155 us (22%)
  local copies, waits for them, and re-layouts  108 us (15%)
  starting transfers between devices  70.1 us (10%)
  other arithmetic  56.4 us (8%)
  between operations  22.2 us (3%)
    all_gather x4, waiting for transfers between devices, inject(): whole_grid = lax.all_gather(section, 'slab', axis=1, tiled=True)  246 us
    all_gather x3, blocking collectives, on_device(): box_strip = lax.all_gather(arrived, 'slab', axis=1, tiled=True)  155 us
    ppermute x25, starting transfers between devices, shifted(): lax.ppermute(value, axis, [(source, source + steps) for source in range(f...  69.9 us
    broadcast_in_dim x18, local copies, waits for them, and re-layouts, upsample(): jnp.broadcast_to(section[:, :, None, :, None, :, None], (components, leng...  63.1 us
    ppermute x25, waiting for transfers between devices, shifted(): lax.ppermute(value, axis, [(source, source + steps) for source in range(f...  27.9 us
    reduce_sum x3, local copies, waits for them, and re-layouts, restrict(): jnp.mean(field.reshape(components, length_x // 3, 3, length_y // 3, 3, le...  20.1 us
    another operation x18, other arithmetic, advance(): jnp.stack([shifted_up(efield_z, 1) - efield_z - (shifted_up(efield_y, 2)...  15.7 us
  transfers between devices with their start and end apart: 29, of which 19 were waited for; matrix products, arithmetic and copies ran while one was open for 14% of the time, Pallas kernels for 0%

commit v1 on v0

v1 whole, which is shorter than its diff:
```python
import functools

import jax
import jax.numpy as jnp
from jax import lax
from jax.experimental import pallas as pl
from jax.experimental.pallas import tpu as pltpu
from jax.sharding import PartitionSpec as P

STEPS = 3
SUBS = 3
PERMITTIVITY = (1.0, 1.5, 1.2, 2.0)
STRENGTH = (0.4, 0.9, 0.3, 1.1)
RESONANCE = (0.6, 0.5, 0.8, 0.3)
DAMPING_RATE = (0.3, 0.2, 0.05, 0.4)
COURANT = 0.5
STEP_COARSE = 0.5
STEP_FINE = STEP_COARSE / 3.0
PLANES = 3
MESH = pl.DeviceIdType.MESH
EXACT = lax.Precision.HIGHEST


def tables(step):
    rows = zip(PERMITTIVITY, STRENGTH, RESONANCE, DAMPING_RATE)
    return [
        (1.0 - step * d, -step * r, step * s * r, COURANT / e, step / e) for e, s, r, d in rows
    ]


def pick(material, values):
    out = jnp.full(material.shape, values[0], jnp.float32)
    for index in range(1, 4):
        out = jnp.where(material == index, jnp.float32(values[index]), out)
    return out


def iota(shape, dim):
    return lax.broadcasted_iota(jnp.int32, shape, dim)


def down_y(u):
    return jnp.where(iota(u.shape, 0) == 0, 0.0, pltpu.roll(u, 1, 0))


def up_y(u):
    last = u.shape[0] - 1
    return jnp.where(iota(u.shape, 0) == last, 0.0, pltpu.roll(u, last, 0))


def down_z(u):
    return jnp.where(iota(u.shape, 1) == 0, 0.0, pltpu.roll(u, 1, 1))


def up_z(u):
    last = u.shape[1] - 1
    return jnp.where(iota(u.shape, 1) == last, 0.0, pltpu.roll(u, last, 1))


def kernel(
    n_slab, width, depth,
    off_ref, e_in, h_in, p_in, j_in, m_in,
    e_out, h_out, p_out, j_out,
    E, H, Q, J, M, CO, C3, m_right, T,
    h_send, h_recv, b_send, b_recv,
    sec_send, sec_recv, up_prev, up_last, mean_send, mean_recv,
    load_sem, out_sem, m_send_sem, m_recv_sem,
    hs_sem, hr_sem, bs_sem, br_sem, ss_sem, sr_sem, ms_sem, mr_sem,
):
    slab = lax.axis_index("slab")
    level = lax.axis_index("grid")
    box_y, box_z = width // 3, depth // 3
    first_slab = n_slab // 8
    is_fine = level == 1
    is_coarse = level == 0
    has_left = slab > 0
    has_right = slab < n_slab - 1
    partner_slab = first_slab + slab // 3
    partner_plane = slab % 3
    fine_at = [3 * (slab - first_slab) + p for p in range(PLANES)]
    in_box = [(f >= 0) & (f < n_slab) for f in fine_at]
    on_box = [is_coarse & b for b in in_box]

    fields = ((e_in, E, e_out), (h_in, H, h_out), (p_in, Q, p_out), (j_in, J, j_out))
    loads = [
        [pltpu.make_async_copy(src.at[0, :, p], dst.at[p], load_sem.at[k, p]) for p in range(PLANES)]
        for k, (src, dst, _) in enumerate(fields)
    ]
    load_m = pltpu.make_async_copy(m_in.at[0], M, load_sem.at[4, 0])

    barrier = pltpu.get_barrier_semaphore()

    def greet(condition, target):
        @pl.when(condition)
        def _():
            pl.semaphore_signal(barrier, inc=1, device_id=target, device_id_type=MESH)

    greet(has_left, {"slab": slab - 1})
    greet(has_right, {"slab": slab + 1})
    greet(is_fine, {"grid": 0, "slab": partner_slab})
    for p in range(PLANES):
        greet(on_box[p], {"grid": 1, "slab": fine_at[p]})

    load_m.start()
    for p in range(PLANES):
        for k in range(4):
            loads[k][p].start()

    greeted = has_left.astype(jnp.int32) + has_right.astype(jnp.int32) + is_fine.astype(jnp.int32)
    for p in range(PLANES):
        greeted = greeted + on_box[p].astype(jnp.int32)

    def remote(src, dst, send, recv, target):
        return pltpu.make_async_remote_copy(
            src_ref=src, dst_ref=dst, send_sem=send, recv_sem=recv, device_id=target, device_id_type=MESH
        )

    def h_copy(slot):
        return remote(h_send.at[slot], h_recv.at[slot], hs_sem.at[slot], hr_sem.at[slot], {"slab": slab + 1})

    def b_copy(slot):
        return remote(b_send.at[slot, 0:2], b_recv.at[slot], bs_sem.at[slot], br_sem.at[slot], {"slab": slab - 1})

    m_copy = remote(m_in.at[0, 0], m_right, m_send_sem, m_recv_sem, {"slab": slab - 1})

    def section_copy(index, p):
        return remote(
            sec_send.at[index, p], sec_recv.at[index], ss_sem.at[index, p], sr_sem.at[index],
            {"grid": 1, "slab": fine_at[p]},
        )

    def section_arrival(index):
        return remote(
            sec_send.at[index, 0], sec_recv.at[index], ss_sem.at[index, 0], sr_sem.at[index],
            {"grid": 0, "slab": partner_slab},
        )

    def mean_copy(index):
        return remote(
            mean_send.at[index], mean_recv.at[index, partner_plane], ms_sem.at[index],
            mr_sem.at[index, partner_plane], {"grid": 0, "slab": partner_slab},
        )

    def mean_arrival(index, p):
        return remote(
            mean_send.at[index], mean_recv.at[index, p], ms_sem.at[index], mr_sem.at[index, p],
            {"grid": 1, "slab": fine_at[p]},
        )

    def oscillate(p):
        a_j, a_p, a_e = CO[0, p], CO[1, p], CO[2, p]
        for c in range(3):
            current = a_j * J[p, c] + a_p * Q[p, c] + a_e * E[p, c]
            J[p, c] = current

    def move(p, step):
        for c in range(3):
            Q[p, c] = Q[p, c] + step * J[p, c]

    def electric(p):
        k_c, k_j = CO[3, p], CO[4, p]
        h_x, h_y, h_z = H[p, 0], H[p, 1], H[p, 2]
        e_x = E[p, 0] - k_j * J[p, 0] + k_c * ((h_z - down_y(h_z)) - (h_y - down_z(h_y)))
        b_y = E[p, 1] - k_j * J[p, 1] + k_c * ((h_x - down_z(h_x)) - h_z)
        b_z = E[p, 2] - k_j * J[p, 2] + k_c * (h_y - (h_x - down_y(h_x)))
        return e_x, b_y, b_z

    def electric_whole(p):
        e_x, b_y, b_z = electric(p)
        k_c = CO[3, p]
        E[p, 0] = e_x
        E[p, 1] = b_y + k_c * H[p - 1, 2]
        E[p, 2] = b_z - k_c * H[p - 1, 1]

    def magnetic(p):
        e_x, e_y, e_z = E[p, 0], E[p, 1], E[p, 2]
        h_x = H[p, 0] - COURANT * ((up_y(e_z) - e_z) - (up_z(e_y) - e_y))
        g_y = H[p, 1] - COURANT * ((up_z(e_x) - e_x) + e_z)
        g_z = H[p, 2] + COURANT * (e_y + (up_y(e_x) - e_x))
        return h_x, g_y, g_z

    def magnetic_whole(p):
        h_x, g_y, g_z = magnetic(p)
        H[p, 0] = h_x
        H[p, 1] = g_y + COURANT * E[p + 1, 2]
        H[p, 2] = g_z - COURANT * E[p + 1, 1]

    def set_coefficients(step):
        load_m.wait()
        values = tables(step)
        for p in range(PLANES):
            material = M[p]
            for k in range(5):
                CO[k, p] = pick(material, [row[k] for row in values])

    def begin(step, first):
        set_coefficients(step)
        for k in range(4):
            loads[k][0].wait()
        loads[1][2].wait()
        first()
        oscillate(0)
        move(0, step)
        e_x, b_y, b_z = electric(0)
        b_send[0, 0], b_send[0, 1], b_send[0, 2] = b_y, b_z, e_x
        h_send[0, 0], h_send[0, 1] = H[2, 1], H[2, 2]

        @pl.when(jnp.logical_not(has_left))
        def _():
            h_recv[...] = jnp.zeros_like(h_recv)

        @pl.when(jnp.logical_not(has_right))
        def _():
            b_recv[...] = jnp.zeros_like(b_recv)
            m_right[...] = jnp.zeros_like(m_right)

        pl.semaphore_wait(barrier, greeted)

        @pl.when(has_right)
        def _():
            h_copy(0).start()

        @pl.when(has_left)
        def _():
            b_copy(0).start()
            m_copy.start()

    def rest_of_loads(skip):
        for k in range(4):
            for p in range(1, PLANES):
                if (k, p) != (1, 2) and k not in skip:
                    loads[k][p].wait()

    def learn_right():
        @pl.when(has_right)
        def _():
            m_copy.wait_recv()

        @pl.when(has_left)
        def _():
            m_copy.wait_send()

        scale = pick(m_right[...], [COURANT / e for e in PERMITTIVITY])
        C3[...] = scale * has_right.astype(jnp.float32)

    def hear_left(slot):
        @pl.when(has_left)
        def _():
            h_copy(slot).wait_recv()

    def hear_right(slot):
        @pl.when(has_right)
        def _():
            b_copy(slot).wait_recv()

    def sent(slot):
        @pl.when(has_right)
        def _():
            h_copy(slot).wait_send()

        @pl.when(has_left)
        def _():
            b_copy(slot).wait_send()

    def last_plane(slot):
        h_x, g_y, g_z = magnetic(2)
        e_y = b_recv[slot, 0] + C3[...] * h_send[slot, 1]
        e_z = b_recv[slot, 1] - C3[...] * h_send[slot, 0]
        H[2, 0] = h_x
        H[2, 1] = g_y + COURANT * e_z
        H[2, 2] = g_z - COURANT * e_y

    def first_plane(slot):
        k_c = CO[3, 0]
        E[0, 0] = b_send[slot, 2]
        E[0, 1] = b_send[slot, 0] + k_c * h_recv[slot, 1]
        E[0, 2] = b_send[slot, 1] - k_c * h_recv[slot, 0]

    def tell_right(slot):
        h_send[slot, 0], h_send[slot, 1] = H[2, 1], H[2, 2]

        @pl.when(has_right)
        def _():
            h_copy(slot).start()

    def tell_left(slot, step):
        oscillate(0)
        move(0, step)
        e_x, b_y, b_z = electric(0)
        b_send[slot, 0], b_send[slot, 1], b_send[slot, 2] = b_y, b_z, e_x

        @pl.when(has_left)
        def _():
            b_copy(slot).start()

    def rim(p):
        row, column = iota((width, depth), 0), iota((width, depth), 1)
        edge = (row == 0) | (row == width - 1) | (column == 0) | (column == depth - 1)
        if p == 0:
            edge = edge | (slab == 0)
        if p == PLANES - 1:
            edge = edge | (slab == n_slab - 1)
        return edge

    def upsampled(index):
        section = sec_recv[index].reshape(3 * box_y, box_z)
        spread_z = (iota((box_z, depth), 1) // 3 == iota((box_z, depth), 0)).astype(jnp.float32)
        spread_y = (iota((3 * width, 3 * box_y), 0) // 3 == iota((3 * width, 3 * box_y), 1)).astype(jnp.float32)
        wide = jnp.dot(section, spread_z, precision=EXACT, preferred_element_type=jnp.float32)
        return jnp.dot(spread_y, wide, precision=EXACT, preferred_element_type=jnp.float32)

    def average():
        total = [E[0, c] + E[1, c] + E[2, c] for c in range(3)]
        total = jnp.concatenate(total, axis=0)
        fold_z = (iota((depth, box_z), 0) // 3 == iota((depth, box_z), 1)).astype(jnp.float32)
        fold_y = (iota((3 * box_y, 3 * width), 1) // 3 == iota((3 * box_y, 3 * width), 0)).astype(jnp.float32)
        rows = jnp.dot(fold_y, total, precision=EXACT, preferred_element_type=jnp.float32)
        both = jnp.dot(rows, fold_z, precision=EXACT, preferred_element_type=jnp.float32)
        return both * jnp.float32(1.0 / 27.0)

    def write(k):
        for p in range(PLANES):
            pltpu.make_async_copy(fields[k][1].at[p], fields[k][2].at[0, :, p], out_sem.at[k, p]).start()

    def written():
        for k in range(4):
            for p in range(PLANES):
                pltpu.make_async_copy(fields[k][1].at[p], fields[k][2].at[0, :, p], out_sem.at[k, p]).wait()

    @pl.when(is_fine)
    def _():
        begin(STEP_FINE, lambda: None)
        rest_of_loads(())
        total_subs = STEPS * SUBS

        def sub_step(m, carry):
            step_index = m // SUBS
            sub_index = m % SUBS
            slot = m % 2
            for p in (1, 2):
                oscillate(p)
                move(p, STEP_FINE)
            electric_whole(2)
            electric_whole(1)
            magnetic_whole(1)

            @pl.when(m == 0)
            def _():
                learn_right()

            hear_right(slot)
            last_plane(slot)

            @pl.when(m < total_subs - 1)
            def _():
                tell_right(1 - slot)

            hear_left(slot)
            first_plane(slot)
            magnetic_whole(0)
            sent(slot)

            @pl.when(m == 0)
            def _():
                section_arrival(0).wait_recv()
                up_last[...] = upsampled(0).reshape(up_last.shape)

            @pl.when(sub_index == 0)
            def _():
                up_prev[...] = up_last[...]
                section_arrival(step_index + 1).wait_recv()
                up_last[...] = upsampled(step_index + 1).reshape(up_last.shape)

            weight = (sub_index + 1).astype(jnp.float32) * jnp.float32(1.0 / 3.0)
            for c in range(3):
                before = up_prev[c]
                boundary = before + weight * (up_last[c] - before)
                for p in range(PLANES):
                    E[p, c] = jnp.where(rim(p), boundary, E[p, c])

            @pl.when(m < total_subs - 1)
            def _():
                tell_left(1 - slot, STEP_FINE)

            @pl.when(sub_index == SUBS - 1)
            def _():
                averaged = average()

                mean_send[step_index] = averaged.reshape(3, box_y, box_z)
                mean_copy(step_index).start()

            return carry

        lax.fori_loop(0, total_subs, sub_step, 0)
        for k in range(4):
            write(k)
        for index in range(STEPS):
            mean_copy(index).wait_send()
        written()

    @pl.when(is_coarse)
    def _():
        corner_y = off_ref[0]

        def take_section(index, source):
            for p in range(PLANES):
                for c in range(3):
                    slice_z = source[p, c, :, depth - box_z : depth]
                    sec_send[index, p, c] = pltpu.roll(slice_z, width - corner_y, 0)[:box_y]

        def send_section(index):
            for p in range(PLANES):

                @pl.when(in_box[p])
                def _(p=p):
                    section_copy(index, p).start()

        def first():
            for p in range(1, PLANES):
                loads[0][p].wait()
            take_section(0, E)

        def place(index):
            row, column = iota((width, box_z), 0), iota((width, box_z), 1)
            interior = (row >= corner_y + 1) & (row <= corner_y + box_y - 2) & (column >= 1) & (column <= box_z - 2)
            for p in range(PLANES):

                @pl.when(in_box[p])
                def _(p=p):
                    mean_arrival(index, p).wait_recv()
                    inside = interior & (fine_at[p] >= 1) & (fine_at[p] <= n_slab - 2)
                    for c in range(3):
                        mean = mean_recv[index, p, c]
                        tall = jnp.concatenate([mean] * (width // box_y), axis=0)
                        placed = pltpu.roll(tall, corner_y, 0)
                        kept = E[p, c, :, depth - box_z : depth]
                        E[p, c, :, depth - box_z : depth] = jnp.where(inside, placed, kept)

        def foresee(slot):
            for p in range(PLANES):
                a_j, a_p, a_e, k_c, k_j = (CO[k, p] for k in range(5))
                h_x, h_y, h_z = H[p, 0], H[p, 1], H[p, 2]
                if p == 0:
                    y_back, z_back = h_recv[slot, 0], h_recv[slot, 1]
                else:
                    y_back, z_back = H[p - 1, 1], H[p - 1, 2]
                curls = (
                    (h_z - down_y(h_z)) - (h_y - down_z(h_y)),
                    (h_x - down_z(h_x)) - (h_z - z_back),
                    (h_y - y_back) - (h_x - down_y(h_x)),
                )
                for c in range(3):
                    current = a_j * J[p, c] + a_p * Q[p, c] + a_e * E[p, c]
                    T[p, c] = E[p, c] - k_j * current + k_c * curls[c]

        begin(STEP_COARSE, first)
        send_section(0)
        rest_of_loads((0,))

        def step(n, carry):
            slot = n % 2
            for p in (1, 2):
                oscillate(p)
                move(p, STEP_COARSE)
            electric_whole(2)
            electric_whole(1)
            magnetic_whole(1)

            @pl.when(n == 0)
            def _():
                learn_right()
                hear_left(0)

            first_plane(slot)

            @pl.when(n == 0)
            def _():
                take_section(1, E)
                send_section(1)

            magnetic_whole(0)
            hear_right(slot)
            last_plane(slot)
            sent(slot)

            @pl.when(n < STEPS - 1)
            def _():
                tell_right(1 - slot)
                hear_left(1 - slot)
                foresee(1 - slot)
                take_section(n + 2, T)
                send_section(n + 2)

            place(n)

            @pl.when(n < STEPS - 1)
            def _():
                tell_left(1 - slot, STEP_COARSE)

            return carry

        lax.fori_loop(0, STEPS, step, 0)
        for k in range(4):
            write(k)
        for index in range(STEPS + 1):
            for p in range(PLANES):

                @pl.when(in_box[p])
                def _(index=index, p=p):
                    section_copy(index, p).wait_send()

        written()


def on_device(n_slab, efield, hfield, polar, current, material, box_offset):
    planes, width, depth = efield.shape[2:]
    box_y, box_z = width // 3, depth // 3
    plane = (width, depth)
    f32 = jnp.float32
    dma = pltpu.SemaphoreType.DMA
    scratch = [
        pltpu.VMEM((planes, 3) + plane, f32),
        pltpu.VMEM((planes, 3) + plane, f32),
        pltpu.VMEM((planes, 3) + plane, f32),
        pltpu.VMEM((planes, 3) + plane, f32),
        pltpu.VMEM((planes,) + plane, jnp.int32),
        pltpu.VMEM((5, planes) + plane, f32),
        pltpu.VMEM(plane, f32),
        pltpu.VMEM(plane, jnp.int32),
        pltpu.VMEM((planes, 3) + plane, f32),
        pltpu.VMEM((2, 2) + plane, f32),
        pltpu.VMEM((2, 2) + plane, f32),
        pltpu.VMEM((2, 3) + plane, f32),
        pltpu.VMEM((2, 2) + plane, f32),
        pltpu.VMEM((STEPS + 1, planes, 3, box_y, box_z), f32),
        pltpu.VMEM((STEPS + 1, 3, box_y, box_z), f32),
        pltpu.VMEM((3,) + plane, f32),
        pltpu.VMEM((3,) + plane, f32),
        pltpu.VMEM((STEPS, 3, box_y, box_z), f32),
        pltpu.VMEM((STEPS, planes, 3, box_y, box_z), f32),
        dma((5, planes)),
        dma((4, planes)),
        dma,
        dma,
        dma((2,)),
        dma((2,)),
        dma((2,)),
        dma((2,)),
        dma((STEPS + 1, planes)),
        dma((STEPS + 1,)),
        dma((STEPS,)),
        dma((STEPS, planes)),
    ]
    whole = pl.BlockSpec(memory_space=pl.ANY)
    return pl.pallas_call(
        functools.partial(kernel, n_slab, width, depth),
        out_shape=[jax.ShapeDtypeStruct(efield.shape, f32)] * 4,
        in_specs=[pl.BlockSpec(memory_space=pltpu.SMEM)] + [whole] * 5,
        out_specs=[whole] * 4,
        scratch_shapes=scratch,
        compiler_params=pltpu.CompilerParams(
            collective_id=1, has_side_effects=True, vmem_limit_bytes=32 * 1024 * 1024
        ),
    )(box_offset, efield, hfield, polar, current, material)


def solution(mesh):
    field = P("grid", "angle", "slab", None, None)
    return jax.shard_map(
        functools.partial(on_device, mesh.shape["slab"]),
        mesh=mesh,
        in_specs=(field, field, field, field, P("grid", "slab", None, None), P()),
        out_specs=(field, field, field, field),
        check_vma=False,
    )
```

time: 700 us -> 72.2 us (0.10)
  the two profiles are of different devices: /device:TPU:99 before, /device:TPU:130 now
where the time goes in v1:
time: 72.2 us; the launch traced here: 71.9 us
  Pallas kernels  62.9 us (87%)
  local copies, waits for them, and re-layouts  8.34 us (12%)
    pallas_call x1, Pallas kernels, on_device(): pl.pallas_call(functools.partial(kernel, n_slab, width, depth), out_shape...  62.9 us
    unnamed x16, local copies, waits for them, and re-layouts  8.34 us

profile of v1, /device:TPU:130, one launch (start us, length us, event | category | flops | bytes accessed | tf_op | source)
XLA Modules:
  0.0 71.9 jit_solution(2859097247241737547)
XLA Ops:
  0.6 0.0 copy-start
  0.6 1.0 %copy-done = f32[1,3,3,24,384]{4,3,2,1,0:T(8,128)S(1)} copy-done((f32[1,3,3,24,384]{4,3,2,1,0:T(8,128)S(1)}, f32[1,3,3,24,384]{4,3,2,1,0:T(8,128)}, u32[]{:S(2)}) %copy-start) | copy-done | bytes 331800
  1.6 0.0 copy-start.1
  1.6 1.0 %copy-done.1 = f32[1,3,3,24,384]{4,3,2,1,0:T(8,128)S(1)} copy-done((f32[1,3,3,24,384]{4,3,2,1,0:T(8,128)S(1)}, f32[1,3,3,24,384]{4,3,2,1,0:T(8,128)}, u32[]{:S(2)}) %copy-start.1) | copy-done | bytes 331800
  2.6 0.0 copy-start.2
  2.6 1.0 %copy-done.2 = f32[1,3,3,24,384]{4,3,2,1,0:T(8,128)S(1)} copy-done((f32[1,3,3,24,384]{4,3,2,1,0:T(8,128)S(1)}, f32[1,3,3,24,384]{4,3,2,1,0:T(8,128)}, u32[]{:S(2)}) %copy-start.2) | copy-done | bytes 331800
  3.6 0.0 copy-start.3
  3.6 1.0 %copy-done.3 = f32[1,3,3,24,384]{4,3,2,1,0:T(8,128)S(1)} copy-done((f32[1,3,3,24,384]{4,3,2,1,0:T(8,128)S(1)}, f32[1,3,3,24,384]{4,3,2,1,0:T(8,128)}, u32[]{:S(2)}) %copy-start.3) | copy-done | bytes 331800
  4.5 0.0 copy-start.4
  4.5 0.9 %copy-done.4 = s32[1,3,24,384]{3,2,1,0:T(8,128)S(1)} copy-done((s32[1,3,24,384]{3,2,1,0:T(8,128)S(1)}, s32[1,3,24,384]{3,2,1,0:T(8,128)}, u32[]{:S(2)}) %copy-start.4) | copy-done | bytes 110616
  5.4 0.0 copy-start.5
  5.4 0.7 copy-done.5
  6.1 62.9 %shard_map.93 = (f32[1,3,3,24,384]{4,3,2,1,0:T(8,128)S(1)}, f32[1,3,3,24,384]{4,3,2,1,0:T(8,128)S(1)}, f32[1,3,3,24,384]{4,3,2,1,0:T(8,128)S(1)}, f32[1,3,3,24,384]{4,3,2,1,0:T(8,128)S(1)}) custom-call(s32[2]{0:T(128)S(1)} %copy-done.5, f32[1,3,3,24,384]{4,3,2,1,0:T(8,128)S(1)} %copy-done, f32[1,3,3,24,384]{4,3,2,1,0:T(8,128)S(1)} %copy-done.1, ...), custom_call_target="tpu_custom_call" | custom-call | tf_op jit(solution)/shard_map/pallas_call | solution.py:555
  69.0 0.7 %copy.14 = f32[1,3,3,24,384]{4,3,2,1,0:T(8,128)} copy(f32[1,3,3,24,384]{4,3,2,1,0:T(8,128)S(1)} %get-tuple-element.8) | data formatting | bytes 663552
  69.8 0.7 %copy.15 = f32[1,3,3,24,384]{4,3,2,1,0:T(8,128)} copy(f32[1,3,3,24,384]{4,3,2,1,0:T(8,128)S(1)} %get-tuple-element.9) | data formatting | bytes 663552
  70.5 0.7 %copy.16 = f32[1,3,3,24,384]{4,3,2,1,0:T(8,128)} copy(f32[1,3,3,24,384]{4,3,2,1,0:T(8,128)S(1)} %get-tuple-element.10) | data formatting | bytes 663552
  71.2 0.7 %copy.17 = f32[1,3,3,24,384]{4,3,2,1,0:T(8,128)} copy(f32[1,3,3,24,384]{4,3,2,1,0:T(8,128)S(1)} %get-tuple-element.11) | data formatting | bytes 663552
Async XLA Ops:
  0.6 1.0 %copy-start = (f32[1,3,3,24,384]{4,3,2,1,0:T(8,128)S(1)}, f32[1,3,3,24,384]{4,3,2,1,0:T(8,128)}, u32[]{:S(2)}) copy-start(f32[1,3,3,24,384]{4,3,2,1,0:T(8,128)} %e_in.1) | copy-start | bytes 995332
  1.6 1.0 %copy-start.1 = (f32[1,3,3,24,384]{4,3,2,1,0:T(8,128)S(1)}, f32[1,3,3,24,384]{4,3,2,1,0:T(8,128)}, u32[]{:S(2)}) copy-start(f32[1,3,3,24,384]{4,3,2,1,0:T(8,128)} %h_in.1) | copy-start | bytes 995332
  2.6 1.0 %copy-start.2 = (f32[1,3,3,24,384]{4,3,2,1,0:T(8,128)S(1)}, f32[1,3,3,24,384]{4,3,2,1,0:T(8,128)}, u32[]{:S(2)}) copy-start(f32[1,3,3,24,384]{4,3,2,1,0:T(8,128)} %p_in.1) | copy-start | bytes 995332
  3.6 1.0 %copy-start.3 = (f32[1,3,3,24,384]{4,3,2,1,0:T(8,128)S(1)}, f32[1,3,3,24,384]{4,3,2,1,0:T(8,128)}, u32[]{:S(2)}) copy-start(f32[1,3,3,24,384]{4,3,2,1,0:T(8,128)} %j_in.1) | copy-start | bytes 995332
  4.5 0.9 %copy-start.4 = (s32[1,3,24,384]{3,2,1,0:T(8,128)S(1)}, s32[1,3,24,384]{3,2,1,0:T(8,128)}, u32[]{:S(2)}) copy-start(s32[1,3,24,384]{3,2,1,0:T(8,128)} %m_in.1) | copy-start | bytes 331780
  5.4 0.7 copy-start.5

commit v2 on v1

v2 whole, which is shorter than its diff:
```python
import functools

import jax
import jax.numpy as jnp
from jax import lax
from jax.experimental import pallas as pl
from jax.experimental.pallas import tpu as pltpu
from jax.sharding import PartitionSpec as P

STEPS = 3
SUBS = 3
PERMITTIVITY = (1.0, 1.5, 1.2, 2.0)
STRENGTH = (0.4, 0.9, 0.3, 1.1)
RESONANCE = (0.6, 0.5, 0.8, 0.3)
DAMPING_RATE = (0.3, 0.2, 0.05, 0.4)
COURANT = 0.5
STEP_COARSE = 0.5
STEP_FINE = STEP_COARSE / 3.0
PLANES = 3
MESH = pl.DeviceIdType.MESH
EXACT = lax.Precision.HIGHEST


def tables(step):
    rows = zip(PERMITTIVITY, STRENGTH, RESONANCE, DAMPING_RATE)
    return [
        (1.0 - step * d, -step * r, step * s * r, COURANT / e, step / e) for e, s, r, d in rows
    ]


def pick(material, values):
    out = jnp.full(material.shape, values[0], jnp.float32)
    for index in range(1, 4):
        out = jnp.where(material == index, jnp.float32(values[index]), out)
    return out


def iota(shape, dim):
    return lax.broadcasted_iota(jnp.int32, shape, dim)


def down_y(u):
    return jnp.where(iota(u.shape, 0) == 0, 0.0, pltpu.roll(u, 1, 0))


def up_y(u):
    last = u.shape[0] - 1
    return jnp.where(iota(u.shape, 0) == last, 0.0, pltpu.roll(u, last, 0))


def down_z(u):
    return jnp.where(iota(u.shape, 1) == 0, 0.0, pltpu.roll(u, 1, 1))


def up_z(u):
    last = u.shape[1] - 1
    return jnp.where(iota(u.shape, 1) == last, 0.0, pltpu.roll(u, last, 1))


def curl_h(h, back=None):
    x, y, z = h
    c_x = (z - down_y(z)) - (y - down_z(y))
    c_y, c_z = -z, y
    if x is not None:
        c_y, c_z = (x - down_z(x)) - z, y - (x - down_y(x))
    if back is not None:
        c_y, c_z = c_y + back[1], c_z - back[0]
    return c_x, c_y, c_z


def curl_e(e, ahead=None):
    x, y, z = e
    c_x = (up_y(z) - z) - (up_z(y) - y)
    c_y, c_z = z, -y
    if x is not None:
        c_y, c_z = (up_z(x) - x) + z, -y - (up_y(x) - x)
    if ahead is not None:
        c_y, c_z = c_y - ahead[1], c_z + ahead[0]
    return c_x, c_y, c_z


def kernel(
    n_slab, width, depth,
    off_ref, e_in, h_in, p_in, j_in, m_in,
    e_out, h_out, p_out, j_out,
    E, H, Q, J, TE, TH, TQ, TJ, M, CO, m_left, m_right, CL, CR,
    AE, AH, AQ, AJ, A1, BE, BH,
    h_send, h_recv, b_send, b_recv,
    sec_send, sec_recv, table_send, table_recv, near_send, near_recv,
    up_prev, up_last, mean_send, mean_recv, f_send, f_recv,
    load_sem, out_sem, m_sem,
    hs_sem, hr_sem, bs_sem, br_sem, ss_sem, sr_sem, ts_sem, tr_sem, ns_sem, nr_sem,
    ms_sem, mr_sem, fs_sem, fr_sem,
):
    slab = lax.axis_index("slab")
    level = lax.axis_index("grid")
    box_y, box_z = width // 3, depth // 3
    first_slab = n_slab // 8
    is_fine = level == 1
    is_coarse = level == 0
    has_left = slab > 0
    has_right = slab < n_slab - 1
    partner_slab = first_slab + slab // 3
    partner_plane = slab % 3
    borrows = partner_plane == 0
    fine_at = [3 * (slab - first_slab) + p for p in range(PLANES + 1)]
    in_box = [(f >= 0) & (f < n_slab) for f in fine_at]

    fields = ((e_in, E, e_out), (h_in, H, h_out), (p_in, Q, p_out), (j_in, J, j_out))
    loads = [
        [pltpu.make_async_copy(src.at[0, :, p], dst.at[p], load_sem.at[k, p]) for p in range(PLANES)]
        for k, (src, dst, _) in enumerate(fields)
    ]
    load_m = pltpu.make_async_copy(m_in.at[0], M, load_sem.at[4, 0])

    barrier = pltpu.get_barrier_semaphore()

    def greet(condition, target):
        @pl.when(condition)
        def _():
            pl.semaphore_signal(barrier, inc=1, device_id=target, device_id_type=MESH)

    def count(*conditions):
        return sum(c.astype(jnp.int32) for c in conditions)

    greet(is_fine, {"grid": 0, "slab": partner_slab})
    greet(is_fine & borrows, {"grid": 0, "slab": partner_slab - 1})
    greet(has_left, {"slab": slab - 1})
    greet(has_right, {"slab": slab + 1})

    load_m.start()
    for p in range(PLANES):
        for k in range(4):
            loads[k][p].start()

    def remote(src, dst, send, recv, target):
        return pltpu.make_async_remote_copy(
            src_ref=src, dst_ref=dst, send_sem=send, recv_sem=recv, device_id=target, device_id_type=MESH
        )

    left, right = {"slab": slab - 1}, {"slab": slab + 1}

    def h_copy(slot):
        return remote(h_send.at[slot], h_recv.at[slot], hs_sem.at[slot], hr_sem.at[slot], right)

    def b_copy(slot):
        return remote(b_send.at[slot, 0:2], b_recv.at[slot], bs_sem.at[slot], br_sem.at[slot], left)

    m_to_left = remote(m_in.at[0, 0:2], m_right, m_sem.at[0], m_sem.at[1], left)
    m_to_right = remote(m_in.at[0, 2], m_left, m_sem.at[2], m_sem.at[3], right)

    def section_copy(index, p):
        return remote(
            sec_send.at[index, p], sec_recv.at[index], ss_sem.at[index, p], sr_sem.at[index],
            {"grid": 1, "slab": fine_at[p]},
        )

    def table_copy(p):
        return remote(
            table_send.at[p], table_recv, ts_sem.at[p], tr_sem, {"grid": 1, "slab": fine_at[p]}
        )

    def near_copy(index):
        return remote(
            near_send.at[index], near_recv.at[index], ns_sem.at[index], nr_sem.at[index],
            {"grid": 1, "slab": fine_at[PLANES]},
        )

    def mean_copy(index):
        return remote(
            mean_send.at[index], mean_recv.at[index, partner_plane], ms_sem.at[index],
            mr_sem.at[index, partner_plane], {"grid": 0, "slab": partner_slab},
        )

    def mean_arrival(index, p):
        return remote(
            mean_send.at[index], mean_recv.at[index, p], ms_sem.at[index], mr_sem.at[index, p],
            {"grid": 1, "slab": fine_at[p]},
        )

    def f_copy(side):
        return remote(f_send, f_recv.at[side], fs_sem.at[side], fr_sem.at[side], right if side == 0 else left)

    def go(condition, *copies):
        @pl.when(condition)
        def _():
            for copy in copies:
                copy.start()

    def heard(condition, *copies):
        @pl.when(condition)
        def _():
            for copy in copies:
                copy.wait_recv()

    def sent(condition, *copies):
        @pl.when(condition)
        def _():
            for copy in copies:
                copy.wait_send()

    def get(ref, *index):
        return tuple(ref[(*index, c)] for c in range(3))

    def put(ref, index, values):
        for c, value in enumerate(values):
            if value is not None:
                ref[(*index, c)] = value

    def oscillate(p, step, state):
        e, _, q, j = state
        a_j, a_p, a_e = CO[0, p], CO[1, p], CO[2, p]
        for c in range(3):
            current = a_j * j[p, c] + a_p * q[p, c] + a_e * e[p, c]
            j[p, c] = current
            q[p, c] = q[p, c] + step * current

    def electric(p, state, back=None):
        e, h, _, j = state
        k_c, k_j = CO[3, p], CO[4, p]
        curl = curl_h(get(h, p), back)
        return tuple(e[p, c] - k_j * j[p, c] + k_c * curl[c] for c in range(3))

    def electric_whole(p, state):
        put(state[0], (p,), electric(p, state, (state[1][p - 1, 1], state[1][p - 1, 2])))

    def magnetic(p, state, ahead=None):
        e, h, _, _ = state
        curl = curl_e(get(e, p), ahead)
        return tuple(h[p, c] - COURANT * curl[c] for c in range(3))

    def magnetic_whole(p, state):
        put(state[1], (p,), magnetic(p, state, (state[0][p + 1, 1], state[0][p + 1, 2])))

    def set_coefficients(step):
        load_m.wait()
        values = tables(step)
        for p in range(PLANES):
            material = M[p]
            for k in range(5):
                CO[k, p] = pick(material, [row[k] for row in values])

    def learn_neighbours(step):
        heard(has_right, m_to_left)
        heard(has_left, m_to_right)
        sent(has_left, m_to_left)
        sent(has_right, m_to_right)
        values = tables(step)
        near, far = m_right[0], m_right[1]
        is_there = has_right.astype(jnp.float32)
        for k in range(5):
            scale = is_there if k == 3 else 1.0
            CR[k] = pick(near, [row[k] for row in values]) * scale
        CR[5] = pick(far, [row[3] for row in values]) * is_there
        CL[...] = pick(m_left[...], [row[3] for row in values]) * has_left.astype(jnp.float32)

    def prepare():
        @pl.when(jnp.logical_not(has_left))
        def _():
            h_recv[...] = jnp.zeros_like(h_recv)
            m_left[...] = jnp.zeros_like(m_left)

        @pl.when(jnp.logical_not(has_right))
        def _():
            b_recv[...] = jnp.zeros_like(b_recv)
            m_right[...] = jnp.zeros_like(m_right)

    def tell_right(slot, y, z):
        h_send[slot, 0], h_send[slot, 1] = y, z
        go(has_right, h_copy(slot))

    def set_b(slot, b):
        b_send[slot, 0], b_send[slot, 1], b_send[slot, 2] = b[1], b[2], b[0]

    def tell_left(slot, b):
        set_b(slot, b)
        go(has_left, b_copy(slot))

    def wait_loads(*which):
        for k, p in which:
            loads[k][p].wait()

    def write(k):
        for p in range(PLANES):
            pltpu.make_async_copy(fields[k][1].at[p], fields[k][2].at[0, :, p], out_sem.at[k, p]).start()

    def written():
        for k in range(4):
            for p in range(PLANES):
                pltpu.make_async_copy(fields[k][1].at[p], fields[k][2].at[0, :, p], out_sem.at[k, p]).wait()

    true = (E, H, Q, J)

    @pl.when(is_fine)
    def _():
        step = STEP_FINE
        row, column = iota((width, depth), 0), iota((width, depth), 1)
        edge = (row == 0) | (row == width - 1) | (column == 0) | (column == depth - 1)
        rims = [edge | (slab == 0), edge, edge | (slab == n_slab - 1)]
        small_row, small_column = iota((box_y, box_z), 0), iota((box_y, box_z), 1)
        f_cells = (
            (small_row >= 1) & (small_row <= box_y - 2) & (small_column >= 1) & (small_column <= box_z - 2)
            & (slab >= 1) & (slab <= n_slab - 2)
        )

        def upsampled(section):
            section = section.reshape(3 * box_y, box_z)
            spread_z = (iota((box_z, depth), 1) // 3 == iota((box_z, depth), 0)).astype(jnp.float32)
            spread_y = (iota((3 * width, 3 * box_y), 0) // 3 == iota((3 * width, 3 * box_y), 1)).astype(jnp.float32)
            wide = jnp.dot(section, spread_z, precision=EXACT, preferred_element_type=jnp.float32)
            tall = jnp.dot(spread_y, wide, precision=EXACT, preferred_element_type=jnp.float32)
            return tall.reshape(3, width, depth)

        def average():
            total = jnp.concatenate([E[0, c] + E[1, c] + E[2, c] for c in range(3)], axis=0)
            fold_z = (iota((depth, box_z), 0) // 3 == iota((depth, box_z), 1)).astype(jnp.float32)
            fold_y = (iota((3 * box_y, 3 * width), 1) // 3 == iota((3 * box_y, 3 * width), 0)).astype(jnp.float32)
            rows = jnp.dot(fold_y, total, precision=EXACT, preferred_element_type=jnp.float32)
            both = jnp.dot(rows, fold_z, precision=EXACT, preferred_element_type=jnp.float32)
            return (both * jnp.float32(1.0 / 27.0)).reshape(3, box_y, box_z)

        def boundary(sub):
            weight = jnp.float32((sub + 1) / 3.0)
            return [up_prev[c] + weight * (up_last[c] - up_prev[c]) for c in range(3)]

        def inject(ref, index, p, values):
            for c in range(3):
                ref[(*index, c)] = jnp.where(rims[p], values[c], ref[(*index, c)])

        def open_block(first_slot):
            oscillate(0, step, true)
            e = electric(0, true)
            put(AE, (), e)
            tell_left(first_slot, e)

        set_coefficients(step)
        wait_loads((0, 0), (1, 0), (2, 0), (3, 0), (1, 2))
        prepare()

        @pl.when(jnp.logical_not(borrows))
        def _():
            near_recv[...] = jnp.zeros_like(near_recv)

        @pl.when(jnp.logical_not(has_left))
        def _():
            f_recv[0] = jnp.zeros_like(f_recv[0])

        @pl.when(jnp.logical_not(has_right))
        def _():
            f_recv[1] = jnp.zeros_like(f_recv[1])

        pl.semaphore_wait(barrier, count(has_left, has_right))
        tell_right(0, H[2, 1], H[2, 2])
        open_block(0)
        go(has_left, m_to_left)
        go(has_right, m_to_right)
        wait_loads(*[(k, p) for k in range(4) for p in (1, 2) if (k, p) != (1, 2)])

        def latest(index):
            heard(True, section_copy(index, 0))
            heard(borrows, near_copy(index))
            k_c = table_recv[3]
            base = sec_recv[index]
            return (
                base[0],
                base[1] + k_c * near_recv[index, 1],
                base[2] - k_c * near_recv[index, 0],
            )

        def feedback_response():
            heard(has_left, f_copy(0))
            heard(has_right, f_copy(1))
            here, before, after = f_send, f_recv.at[0], f_recv.at[1]
            curl = curl_e((here[0], here[1], here[2]), (after[1], after[2]))
            back_x = (up_z(before[0]) - before[0], up_y(before[0]) - before[0])
            back_y = back_x[0] - (here[2] - before[2])
            back_z = (here[1] - before[1]) - back_x[1]
            twice = curl_h(curl, (back_y, back_z))
            return [-COURANT * table_recv[3] * t for t in twice]

        def block(b, carry):
            s0 = 3 * b
            for p in (1, 2):
                oscillate(p, step, true)
            electric_whole(2, true)
            electric_whole(1, true)
            h = magnetic(2, true)
            put(BH, (), h)
            tell_right(s0 + 1, h[1], h[2])
            magnetic_whole(1, true)
            curl = curl_e(get(AE), (E[1, 1], E[1, 2]))
            put(AH, (), [H[0, c] - COURANT * curl[c] for c in range(3)])

            @pl.when(b == 0)
            def _():
                heard(True, table_copy(0))
                up_last[...] = upsampled(table_recv[0:3])

            up_prev[...] = up_last[...]
            arrived = latest(b)

            @pl.when(b < STEPS - 1)
            def _():
                up_last[...] = upsampled(jnp.stack(arrived))

            @pl.when(b == STEPS - 1)
            def _():
                extra = feedback_response()
                up_last[...] = upsampled(jnp.stack([a + e for a, e in zip(arrived, extra)]))

            values = boundary(0)
            inject(AE, (), 0, values)
            inject(E, (1,), 1, values)
            inject(E, (2,), 2, values)
            a_j, a_p, a_e, k_c, k_j = (CO[k, 0] for k in range(5))
            for c in range(3):
                current = a_j * J[0, c] + a_p * Q[0, c] + a_e * AE[c]
                AJ[c] = current
                AQ[c] = Q[0, c] + step * current
            curl = curl_h(get(AH))
            e_0 = tuple(AE[c] - k_j * AJ[c] + k_c * curl[c] for c in range(3))
            put(AE, (), e_0)
            tell_left(s0 + 1, e_0)
            for p in (1, 2):
                oscillate(p, step, true)
            curl = curl_h(get(BH), (H[1, 1], H[1, 2]))
            e_2 = tuple(E[2, c] - CO[4, 2] * J[2, c] + CO[3, 2] * curl[c] for c in range(3))
            put(BE, (), e_2)
            curl = curl_e(e_2)
            h = tuple(BH[c] - COURANT * curl[c] for c in range(3))
            put(BH, (), h)
            tell_right(s0 + 2, h[1], h[2])
            curl = curl_h(get(H, 1), (AH[1], AH[2]))
            e_1 = tuple(E[1, c] - CO[4, 1] * J[1, c] + CO[3, 1] * curl[c] for c in range(3))
            put(A1, (), e_1)
            curl = curl_e(get(AE), (A1[1], A1[2]))
            put(AH, (), [AH[c] - COURANT * curl[c] for c in range(3)])
            values = boundary(1)
            inject(AE, (), 0, values)
            for c in range(3):
                current = a_j * AJ[c] + a_p * AQ[c] + a_e * AE[c]
                AJ[c] = current
                AQ[c] = AQ[c] + step * current
            curl = curl_h(get(AH))
            e_0 = tuple(AE[c] - k_j * AJ[c] + k_c * curl[c] for c in range(3))
            put(AE, (), e_0)
            tell_left(s0 + 2, e_0)

            @pl.when(b == 0)
            def _():
                learn_neighbours(step)

            def face(coefficients, k_near, k_back, there, h_own, e_own, hear):
                a_j, a_p, a_e, k_c, k_j = coefficients
                side = COURANT * there.astype(jnp.float32)

                def kept(u):
                    return jnp.where(edge, 0.0, u)

                hear(0)
                h_y, h_z = h_own(0)
                e_y, e_z = e_own(0)
                d_y, d_z = k_c * h_z, -k_c * h_y
                e_y, e_z = e_y + d_y, e_z + d_z
                l_y, l_z = side * e_z, -side * e_y
                d_h = tuple(-COURANT * u for u in curl_e((None, d_y, d_z)))
                d_y, d_z = kept(d_y), kept(d_z)
                j_y, j_z = a_e * d_y, a_e * d_z
                p_y, p_z = step * j_y, step * j_z
                hear(1)
                h_y, h_z = h_own(1)
                e_y, e_z = e_own(1)
                h_y, h_z = h_y + l_y, h_z + l_z
                curl = curl_h(d_h, (h_y, h_z))
                d_x = k_c * curl[0]
                d_y = d_y - k_j * j_y + k_c * curl[1]
                d_z = d_z - k_j * j_z + k_c * curl[2]
                e_y, e_z = e_y + d_y, e_z + d_z
                l_e = tuple(k_back * u for u in curl_h((None, l_y, l_z)))
                curl = curl_e(l_e)
                l_h = (
                    -COURANT * curl[0],
                    l_y - COURANT * curl[1] + side * e_z,
                    l_z - COURANT * curl[2] - side * e_y,
                )
                f_y, f_z = k_near * d_h[2], -k_near * d_h[1]
                curl = curl_e((d_x, d_y, d_z), (f_y, f_z))
                d_h = tuple(d_h[c] - COURANT * curl[c] for c in range(3))
                d_e = kept(d_x), kept(d_y), kept(d_z)
                d_j = (a_e * d_e[0], a_j * j_y + a_p * p_y + a_e * d_e[1], a_j * j_z + a_p * p_z + a_e * d_e[2])
                d_p = (step * d_j[0], p_y + step * d_j[1], p_z + step * d_j[2])
                curl = curl_h(d_h, (l_h[1], l_h[2]))
                d_e = tuple(d_e[c] - k_j * d_j[c] + k_c * curl[c] for c in range(3))
                return d_e, d_j, d_p, d_h, (f_y, f_z), l_e, l_h

            def hear_left(m):
                heard(has_left, h_copy(s0 + m))

            def hear_right(m):
                heard(has_right, b_copy(s0 + m))

            d_e, _, _, _, _, l_e, l_h = face(
                [CR[k] for k in range(5)], CR[5], CO[3, 2], has_right,
                lambda m: (h_send[s0 + m, 0], h_send[s0 + m, 1]),
                lambda m: (b_recv[s0 + m, 0], b_recv[s0 + m, 1]),
                hear_right,
            )
            k_c = CR[3]
            next_y = d_e[1] + k_c * h_send[s0 + 2, 1]
            next_z = d_e[2] - k_c * h_send[s0 + 2, 0]
            put(H, (2,), [BH[c] + l_h[c] for c in range(3)])
            put(E, (2,), [BE[c] + l_e[c] for c in range(3)])
            d_e, d_j, d_p, d_h, near, _, _ = face(
                [CO[k, 0] for k in range(5)], CO[3, 1], CL[...], has_left,
                lambda m: (h_recv[s0 + m, 0], h_recv[s0 + m, 1]),
                lambda m: (b_send[s0 + m, 0], b_send[s0 + m, 1]),
                hear_left,
            )
            put(H, (0,), [AH[c] + d_h[c] for c in range(3)])
            put(J, (0,), [AJ[c] + d_j[c] for c in range(3)])
            put(Q, (0,), [AQ[c] + d_p[c] for c in range(3)])
            put(AE, (), [AE[c] + d_e[c] for c in range(3)])
            put(E, (1,), [A1[0], A1[1] + near[0], A1[2] + near[1]])

            magnetic_whole(1, true)
            values = boundary(1)
            for p in (1, 2):
                inject(E, (p,), p, values)
                oscillate(p, step, true)
            electric_whole(2, true)
            electric_whole(1, true)
            magnetic_whole(1, true)
            values = boundary(2)

            hear_right(2)
            put(H, (2,), magnetic(2, true, (next_y + b_recv[s0 + 2, 0], next_z + b_recv[s0 + 2, 1])))

            @pl.when(b < STEPS - 1)
            def _():
                tell_right(s0 + 3, H[2, 1], H[2, 2])

            hear_left(2)
            k_c = CO[3, 0]
            E[0, 0] = AE[0]
            E[0, 1] = AE[1] + k_c * h_recv[s0 + 2, 1]
            E[0, 2] = AE[2] - k_c * h_recv[s0 + 2, 0]
            magnetic_whole(0, true)
            inject(E, (0,), 0, values)

            @pl.when(b < STEPS - 1)
            def _():
                open_block(s0 + 3)

            inject(E, (1,), 1, values)
            inject(E, (2,), 2, values)
            mean = average()
            mean_send[b] = mean
            mean_copy(b).start()

            @pl.when(b == 0)
            def _():
                g = table_recv[4]
                for c in range(3):
                    f_send[c] = jnp.where(f_cells, g * mean[c], 0.0)
                go(has_right, f_copy(0))
                go(has_left, f_copy(1))

            return carry

        lax.fori_loop(0, STEPS, block, 0)
        for k in range(4):
            write(k)
        for slot in range(STEPS * SUBS):
            sent(has_right, h_copy(slot))
            sent(has_left, b_copy(slot))
        sent(has_right, f_copy(0))
        sent(has_left, f_copy(1))
        for index in range(STEPS):
            mean_copy(index).wait_send()
        written()

    @pl.when(is_coarse)
    def _():
        step = STEP_COARSE
        corner_y = off_ref[0]
        guess = (TE, TH, TQ, TJ)

        def cut(value):
            return pltpu.roll(value[:, depth - box_z : depth], width - corner_y, 0)[:box_y]

        row, column = iota((width, box_z), 0), iota((width, box_z), 1)
        interior = (row >= corner_y + 1) & (row <= corner_y + box_y - 2) & (column >= 1) & (column <= box_z - 2)

        def inside(p):
            return interior & (fine_at[p] >= 1) & (fine_at[p] <= n_slab - 2)

        def place(index):
            for p in range(PLANES):

                @pl.when(in_box[p])
                def _(p=p):
                    mean_arrival(index, p).wait_recv()
                    for c in range(3):
                        tall = jnp.concatenate([mean_recv[index, p, c]] * (width // box_y), axis=0)
                        placed = pltpu.roll(tall, corner_y, 0)
                        kept = E[p, c, :, depth - box_z : depth]
                        E[p, c, :, depth - box_z : depth] = jnp.where(inside(p), placed, kept)

        def take(index, p, values):
            for c in range(3):
                sec_send[index, p, c] = cut(values[c])

        def take_near(index, state):
            for c in range(2):
                near_send[index, c] = cut(state[1][2, 1 + c])

        def send(index):
            for p in range(PLANES):
                go(in_box[p], section_copy(index, p))
            go(in_box[PLANES], near_copy(index))

        def first_half(state, slot_h, slot_b):
            e, h, _, _ = state
            for p in (1, 2):
                oscillate(p, step, state)
            electric_whole(2, state)
            electric_whole(1, state)
            k_c = CO[3, 0]
            e[0, 0] = b_send[slot_b, 2]
            e[0, 1] = b_send[slot_b, 0] + k_c * h_recv[slot_h, 1]
            e[0, 2] = b_send[slot_b, 1] - k_c * h_recv[slot_h, 0]
            magnetic_whole(1, state)
            magnetic_whole(0, state)

        def second_half(state, slot_h, slot_b):
            heard(has_right, b_copy(slot_b))
            k_c = CR[3]
            ahead = (
                b_recv[slot_b, 0] + k_c * h_send[slot_h, 1],
                b_recv[slot_b, 1] - k_c * h_send[slot_h, 0],
            )
            put(state[1], (2,), magnetic(2, state, ahead))

        set_coefficients(step)
        wait_loads(*[(k, p) for k in range(4) for p in range(PLANES)])
        for p in range(PLANES):
            for c in range(3):
                table_send[p, c] = cut(E[p, c])
            table_send[p, 3] = cut(CO[3, p])
            table_send[p, 4] = 1.0 - cut(CO[4, p]) * cut(CO[2, p])
        h_send[0, 0], h_send[0, 1] = H[2, 1], H[2, 2]
        take_near(0, true)
        for p in range(PLANES):
            oscillate(p, step, true)
        start = electric(0, true)
        set_b(0, start)
        take(0, 0, start)
        electric_whole(2, true)
        electric_whole(1, true)
        for p in (1, 2):
            take(0, p, get(E, p))
        prepare()
        pl.semaphore_wait(barrier, count(has_left, has_right, *in_box))
        for p in range(PLANES):
            go(in_box[p], table_copy(p), section_copy(0, p))
        go(in_box[PLANES], near_copy(0))
        go(has_right, h_copy(0), m_to_right)
        go(has_left, b_copy(0), m_to_left)

        magnetic_whole(1, true)
        learn_neighbours(step)
        heard(has_left, h_copy(0))
        k_c = CO[3, 0]
        E[0, 0] = start[0]
        E[0, 1] = b_send[0, 0] + k_c * h_recv[0, 1]
        E[0, 2] = b_send[0, 1] - k_c * h_recv[0, 0]
        magnetic_whole(0, true)
        second_half(true, 0, 0)
        tell_right(1, H[2, 1], H[2, 2])

        take_near(1, true)
        for p in range(PLANES):
            for c in range(3):
                value = E[p, c]
                TE[p, c] = value
                kept = value[:, depth - box_z : depth]
                TE[p, c, :, depth - box_z : depth] = jnp.where(inside(p) & in_box[p], 0.0, kept)
                TH[p, c] = H[p, c]
                TQ[p, c] = Q[p, c]
                TJ[p, c] = J[p, c]
        oscillate(0, step, guess)
        start = electric(0, guess)
        tell_left(1, start)
        take(1, 0, start)
        for p in (1, 2):
            oscillate(p, step, guess)
        electric_whole(2, guess)
        electric_whole(1, guess)
        for p in (1, 2):
            take(1, p, get(TE, p))
        send(1)
        heard(has_left, h_copy(1))
        k_c = CO[3, 0]
        TE[0, 0] = b_send[1, 2]
        TE[0, 1] = b_send[1, 0] + k_c * h_recv[1, 1]
        TE[0, 2] = b_send[1, 1] - k_c * h_recv[1, 0]
        magnetic_whole(1, guess)
        magnetic_whole(0, guess)
        second_half(guess, 1, 1)
        take_near(2, guess)
        for p in range(PLANES):
            oscillate(p, step, guess)
            back = None if p == 0 else (TH[p - 1, 1], TH[p - 1, 2])
            take(2, p, electric(p, guess, back))
        send(2)

        place(0)
        oscillate(0, step, true)
        tell_left(2, electric(0, true))
        first_half(true, 1, 2)
        second_half(true, 1, 2)
        tell_right(2, H[2, 1], H[2, 2])
        place(1)
        oscillate(0, step, true)
        tell_left(3, electric(0, true))
        heard(has_left, h_copy(2))
        first_half(true, 2, 3)
        write(2)
        write(3)
        second_half(true, 2, 3)
        write(1)
        place(2)
        write(0)
        for slot in range(3):
            sent(has_right, h_copy(slot))
        for slot in range(4):
            sent(has_left, b_copy(slot))
        for p in range(PLANES):
            sent(in_box[p], table_copy(p), *[section_copy(index, p) for index in range(STEPS)])
        sent(in_box[PLANES], *[near_copy(index) for index in range(STEPS)])
        written()


def hand_over(*refs):
    for source, target in zip(refs[:4], refs[4:]):
        target[...] = source[...]


def on_device(n_slab, efield, hfield, polar, current, material, box_offset):
    planes, width, depth = efield.shape[2:]
    box = (width // 3, depth // 3)
    plane = (width, depth)
    f32 = jnp.float32
    dma = pltpu.SemaphoreType.DMA
    slots = STEPS * SUBS

    def room(*shape, dtype=f32):
        return pltpu.VMEM(shape, dtype)

    state = room(planes, 3, *plane)
    triple = room(3, *plane)
    scratch = [state] * 8 + [
        room(planes, *plane, dtype=jnp.int32),
        room(5, planes, *plane),
        room(*plane, dtype=jnp.int32),
        room(2, *plane, dtype=jnp.int32),
        room(*plane),
        room(6, *plane),
    ]
    scratch += [triple] * 7
    scratch += [room(slots, 2, *plane), room(slots, 2, *plane), room(slots, 3, *plane), room(slots, 2, *plane)]
    scratch += [
        room(STEPS, planes, 3, *box),
        room(STEPS, 3, *box),
        room(planes, 5, *box),
        room(5, *box),
        room(STEPS, 2, *box),
        room(STEPS, 2, *box),
        triple,
        triple,
        room(STEPS, 3, *box),
        room(STEPS, planes, 3, *box),
        room(3, *box),
        room(2, 3, *box),
    ]
    scratch += [dma((5, planes)), dma((4, planes)), dma((4,))]
    scratch += [dma((slots,))] * 4
    scratch += [dma((STEPS, planes)), dma((STEPS,)), dma((planes,)), dma, dma((STEPS,)), dma((STEPS,))]
    scratch += [dma((STEPS,)), dma((STEPS, planes)), dma((2,)), dma((2,))]
    whole = pl.BlockSpec(memory_space=pl.ANY)
    fields = [jax.ShapeDtypeStruct(efield.shape, f32)] * 4
    state = pl.pallas_call(
        functools.partial(kernel, n_slab, width, depth),
        out_shape=fields,
        in_specs=[pl.BlockSpec(memory_space=pltpu.SMEM)] + [whole] * 5,
        out_specs=[whole] * 4,
        scratch_shapes=scratch,
        compiler_params=pltpu.CompilerParams(
            collective_id=1, has_side_effects=True, vmem_limit_bytes=60 * 1024 * 1024
        ),
    )(box_offset, efield, hfield, polar, current, material)
    return pl.pallas_call(
        hand_over,
        out_shape=fields,
        in_specs=[pl.BlockSpec(memory_space=pltpu.VMEM)] * 4,
        out_specs=[pl.BlockSpec(memory_space=pltpu.VMEM)] * 4,
    )(*state)


def solution(mesh):
    field = P("grid", "angle", "slab", None, None)
    return jax.shard_map(
        functools.partial(on_device, mesh.shape["slab"]),
        mesh=mesh,
        in_specs=(field, field, field, field, P("grid", "slab", None, None), P()),
        out_specs=(field, field, field, field),
        check_vma=False,
    )
```

time: 72.2 us -> 42.5 us (0.59)
  the two profiles are of different devices: /device:TPU:130 before, /device:TPU:99 now
where the time goes in v2:
time: 42.5 us; the launch traced here: 42 us
  Pallas kernels  41.3 us (97%)
  between operations  0.64 us (2%)
    pallas_call x1, Pallas kernels, on_device(): pl.pallas_call(functools.partial(kernel, n_slab, width, depth), out_shape...  39 us
    pallas_call x1, Pallas kernels, on_device(): pl.pallas_call(hand_over, out_shape=fields, in_specs=[pl.BlockSpec(memory...  2.35 us

profile of v2, /device:TPU:99, one launch (start us, length us, event | category | flops | bytes accessed | tf_op | source)
XLA Modules:
  0.0 42.0 jit_solution(10958174566916462588)
XLA Ops:
  0.6 39.0 %shard_map.93 = (f32[1,3,3,24,384]{4,3,2,1,0:T(8,128)}, f32[1,3,3,24,384]{4,3,2,1,0:T(8,128)}, f32[1,3,3,24,384]{4,3,2,1,0:T(8,128)}, f32[1,3,3,24,384]{4,3,2,1,0:T(8,128)}) custom-call(s32[2]{0:T(128)} %off_ref.1, f32[1,3,3,24,384]{4,3,2,1,0:T(8,128)} %e_in.1, f32[1,3,3,24,384]{4,3,2,1,0:T(8,128)} %h_in.1, f32[1,3,3,24,384]{4,3,2,1,0:T(8,128)} %p_in.1, ...), custom_call_target="tpu_custom_call" | custom-call | tf_op jit(solution)/shard_map/pallas_call | solution.py:792
  39.6 2.4 %shard_map.94 = (f32[1,3,3,24,384]{4,3,2,1,0:T(8,128)}, f32[1,3,3,24,384]{4,3,2,1,0:T(8,128)}, f32[1,3,3,24,384]{4,3,2,1,0:T(8,128)}, f32[1,3,3,24,384]{4,3,2,1,0:T(8,128)}) custom-call(f32[1,3,3,24,384]{4,3,2,1,0:T(8,128)} %get-tuple-element.8.refs_0_, f32[1,3,3,24,384]{4,3,2,1,0:T(8,128)} %get-tuple-element.9.refs_1_, ...), custom_call_target="tpu_custom_call" | custom-call | tf_op jit(solution)/shard_map/pallas_call | solution.py:802

commit v3 on v2

--- a/solution.py
+++ b/solution.py
@@ -81,14 +81,14 @@
 
 def kernel(
     n_slab, width, depth,
-    off_ref, e_in, h_in, p_in, j_in, m_in,
-    e_out, h_out, p_out, j_out,
-    E, H, Q, J, TE, TH, TQ, TJ, M, CO, m_left, m_right, CL, CR,
-    AE, AH, AQ, AJ, A1, BE, BH,
+    off_in, e_in, h_in, p_in, j_in, m_in,
+    e_out, h_out, p_out, j_out, mean_out,
+    off_ref, E, H, Q, J, TE, TH, TQ, TJ, M, CO, m_left, m_right, CL, CR,
+    AE, AH, AQ, AJ, A1, BE, BH, partial,
     h_send, h_recv, b_send, b_recv,
     sec_send, sec_recv, table_send, table_recv, near_send, near_recv,
     up_prev, up_last, mean_send, mean_recv, f_send, f_recv,
-    load_sem, out_sem, m_sem,
+    off_sem, load_sem, out_sem, m_sem,
     hs_sem, hr_sem, bs_sem, br_sem, ss_sem, sr_sem, ts_sem, tr_sem, ns_sem, nr_sem,
     ms_sem, mr_sem, fs_sem, fr_sem,
 ):
@@ -167,14 +167,16 @@
         )
 
     def mean_copy(index):
+        room = mean_out if index == STEPS - 1 else mean_recv.at[index]
         return remote(
-            mean_send.at[index], mean_recv.at[index, partner_plane], ms_sem.at[index],
+            mean_send.at[index], room.at[partner_plane], ms_sem.at[index],
             mr_sem.at[index, partner_plane], {"grid": 0, "slab": partner_slab},
         )
 
     def mean_arrival(index, p):
+        room = mean_out if index == STEPS - 1 else mean_recv.at[index]
         return remote(
-            mean_send.at[index], mean_recv.at[index, p], ms_sem.at[index], mr_sem.at[index, p],
+            mean_send.at[index], room.at[p], ms_sem.at[index], mr_sem.at[index, p],
             {"grid": 1, "slab": fine_at[p]},
         )
 
@@ -303,20 +305,33 @@
             & (slab >= 1) & (slab <= n_slab - 2)
         )
 
+        def groups(few, many, many_dim):
+            shape = (few, many) if many_dim == 1 else (many, few)
+            same = iota(shape, many_dim) // 3 == iota(shape, 1 - many_dim)
+            return jnp.where(same, 1.0, 0.0).astype(jnp.bfloat16)
+
+        def times(wide, matrix):
+            return sum(jnp.dot(t, matrix, preferred_element_type=jnp.float32) for t in terms(wide))
+
+        def times_left(matrix, wide):
+            return sum(jnp.dot(matrix, t, preferred_element_type=jnp.float32) for t in terms(wide))
+
+        def terms(value):
+            out = []
+            for _ in range(3):
+                out.append(value.astype(jnp.bfloat16))
+                value = value - out[-1].astype(jnp.float32)
+            return out
+
         def upsampled(section):
             section = section.reshape(3 * box_y, box_z)
-            spread_z = (iota((box_z, depth), 1) // 3 == iota((box_z, depth), 0)).astype(jnp.float32)
-            spread_y = (iota((3 * width, 3 * box_y), 0) // 3 == iota((3 * width, 3 * box_y), 1)).astype(jnp.float32)
-            wide = jnp.dot(section, spread_z, precision=EXACT, preferred_element_type=jnp.float32)
-            tall = jnp.dot(spread_y, wide, precision=EXACT, preferred_element_type=jnp.float32)
-            return tall.reshape(3, width, depth)
+            wide = times(section, groups(box_z, depth, 1))
+            return times_left(groups(3 * box_y, 3 * width, 0), wide).reshape(3, width, depth)
 
         def average():
-            total = jnp.concatenate([E[0, c] + E[1, c] + E[2, c] for c in range(3)], axis=0)
-            fold_z = (iota((depth, box_z), 0) // 3 == iota((depth, box_z), 1)).astype(jnp.float32)
-            fold_y = (iota((3 * box_y, 3 * width), 1) // 3 == iota((3 * box_y, 3 * width), 0)).astype(jnp.float32)
-            rows = jnp.dot(fold_y, total, precision=EXACT, preferred_element_type=jnp.float32)
-            both = jnp.dot(rows, fold_z, precision=EXACT, preferred_element_type=jnp.float32)
+            total = jnp.concatenate([E[0, c] + partial[c] for c in range(3)], axis=0)
+            rows = times_left(groups(3 * box_y, 3 * width, 1), total)
+            both = times(rows, groups(box_z, depth, 0))
             return (both * jnp.float32(1.0 / 27.0)).reshape(3, box_y, box_z)
 
         def boundary(sub):
@@ -531,12 +546,21 @@
             electric_whole(1, true)
             magnetic_whole(1, true)
             values = boundary(2)
-
-            hear_right(2)
-            put(H, (2,), magnetic(2, true, (next_y + b_recv[s0 + 2, 0], next_z + b_recv[s0 + 2, 1])))
+            put(H, (2,), magnetic(2, true))
+            near_y, near_z = E[1, 1], E[1, 2]
+            for p in (1, 2):
+                inject(E, (p,), p, values)
+            for c in range(3):
+                partial[c] = E[1, c] + E[2, c]
+
+            def close_right():
+                hear_right(2)
+                H[2, 1] = H[2, 1] + COURANT * (next_z + b_recv[s0 + 2, 1])
+                H[2, 2] = H[2, 2] - COURANT * (next_y + b_recv[s0 + 2, 0])
 
             @pl.when(b < STEPS - 1)
             def _():
+                close_right()
                 tell_right(s0 + 3, H[2, 1], H[2, 2])
 
             hear_left(2)
@@ -544,18 +568,22 @@
             E[0, 0] = AE[0]
             E[0, 1] = AE[1] + k_c * h_recv[s0 + 2, 1]
             E[0, 2] = AE[2] - k_c * h_recv[s0 + 2, 0]
-            magnetic_whole(0, true)
+            put(H, (0,), magnetic(0, true, (near_y, near_z)))
             inject(E, (0,), 0, values)
 
             @pl.when(b < STEPS - 1)
             def _():
                 open_block(s0 + 3)
 
-            inject(E, (1,), 1, values)
-            inject(E, (2,), 2, values)
             mean = average()
             mean_send[b] = mean
-            mean_copy(b).start()
+            for index in range(STEPS):
+
+                @pl.when(b == index)
+                def _(index=index):
+                    mean_copy(index).start()
+
+            pl.when(b == STEPS - 1)(close_right)
 
             @pl.when(b == 0)
             def _():
@@ -582,6 +610,9 @@
     @pl.when(is_coarse)
     def _():
         step = STEP_COARSE
+        load_off = pltpu.make_async_copy(off_in, off_ref, off_sem)
+        load_off.start()
+        load_off.wait()
         corner_y = off_ref[0]
         guess = (TE, TH, TQ, TJ)
 
@@ -727,10 +758,9 @@
         first_half(true, 2, 3)
         write(2)
         write(3)
+        write(0)
         second_half(true, 2, 3)
         write(1)
-        place(2)
-        write(0)
         for slot in range(3):
             sent(has_right, h_copy(slot))
         for slot in range(4):
@@ -739,11 +769,47 @@
             sent(in_box[p], table_copy(p), *[section_copy(index, p) for index in range(STEPS)])
         sent(in_box[PLANES], *[near_copy(index) for index in range(STEPS)])
         written()
-
-
-def hand_over(*refs):
-    for source, target in zip(refs[:4], refs[4:]):
-        target[...] = source[...]
+        for p in range(PLANES):
+            heard(in_box[p], mean_arrival(STEPS - 1, p))
+
+
+def hand_over(n_slab, width, depth, off_in, mean_in, *refs):
+    sources, targets = refs[:4], refs[4:8]
+    off_ref, mean, held, load_sem, out_sem = refs[8:]
+    loads = [pltpu.make_async_copy(sources[k].at[0], held.at[k], load_sem.at[k]) for k in range(4)]
+    stores = [pltpu.make_async_copy(held.at[k], targets[k].at[0], out_sem.at[k]) for k in range(4)]
+    load_off = pltpu.make_async_copy(off_in, off_ref, load_sem.at[4])
+    load_mean = pltpu.make_async_copy(mean_in, mean, load_sem.at[5])
+    load_off.start()
+    load_mean.start()
+    for load in loads:
+        load.start()
+    slab = lax.axis_index("slab")
+    is_coarse = lax.axis_index("grid") == 0
+    box_y, box_z = width // 3, depth // 3
+    load_off.wait()
+    load_mean.wait()
+    corner_y = off_ref[0]
+    row, column = iota((width, box_z), 0), iota((width, box_z), 1)
+    interior = (row >= corner_y + 1) & (row <= corner_y + box_y - 2) & (column >= 1) & (column <= box_z - 2)
+    loads[0].wait()
+    for p in range(PLANES):
+        fine = 3 * (slab - n_slab // 8) + p
+
+        @pl.when(is_coarse & (fine >= 1) & (fine <= n_slab - 2))
+        def _(p=p):
+            for c in range(3):
+                tall = jnp.concatenate([mean[p, c]] * (width // box_y), axis=0)
+                placed = pltpu.roll(tall, corner_y, 0)
+                kept = held[0, c, p, :, depth - box_z : depth]
+                held[0, c, p, :, depth - box_z : depth] = jnp.where(interior, placed, kept)
+
+    stores[0].start()
+    for k in (1, 2, 3):
+        loads[k].wait()
+        stores[k].start()
+    for store in stores:
+        store.wait()
 
 
 def on_device(n_slab, efield, hfield, polar, current, material, box_offset):
@@ -759,7 +825,7 @@
 
     state = room(planes, 3, *plane)
     triple = room(3, *plane)
-    scratch = [state] * 8 + [
+    scratch = [pltpu.SMEM((2,), jnp.int32)] + [state] * 8 + [
         room(planes, *plane, dtype=jnp.int32),
         room(5, planes, *plane),
         room(*plane, dtype=jnp.int32),
@@ -767,7 +833,7 @@
         room(*plane),
         room(6, *plane),
     ]
-    scratch += [triple] * 7
+    scratch += [triple] * 8
     scratch += [room(slots, 2, *plane), room(slots, 2, *plane), room(slots, 3, *plane), room(slots, 2, *plane)]
     scratch += [
         room(STEPS, planes, 3, *box),
@@ -779,11 +845,11 @@
         triple,
         triple,
         room(STEPS, 3, *box),
-        room(STEPS, planes, 3, *box),
+        room(STEPS - 1, planes, 3, *box),
         room(3, *box),
         room(2, 3, *box),
     ]
-    scratch += [dma((5, planes)), dma((4, planes)), dma((4,))]
+    scratch += [dma, dma((5, planes)), dma((4, planes)), dma((4,))]
     scratch += [dma((slots,))] * 4
     scratch += [dma((STEPS, planes)), dma((STEPS,)), dma((planes,)), dma, dma((STEPS,)), dma((STEPS,))]
     scratch += [dma((STEPS,)), dma((STEPS, planes)), dma((2,)), dma((2,))]
@@ -791,20 +857,29 @@
     fields = [jax.ShapeDtypeStruct(efield.shape, f32)] * 4
     state = pl.pallas_call(
         functools.partial(kernel, n_slab, width, depth),
-        out_shape=fields,
-        in_specs=[pl.BlockSpec(memory_space=pltpu.SMEM)] + [whole] * 5,
-        out_specs=[whole] * 4,
+        out_shape=fields + [jax.ShapeDtypeStruct((planes, 3, *box), f32)],
+        in_specs=[whole] * 6,
+        out_specs=[whole] * 5,
         scratch_shapes=scratch,
         compiler_params=pltpu.CompilerParams(
             collective_id=1, has_side_effects=True, vmem_limit_bytes=60 * 1024 * 1024
         ),
     )(box_offset, efield, hfield, polar, current, material)
+    *state, mean = state
     return pl.pallas_call(
-        hand_over,
+        functools.partial(hand_over, n_slab, width, depth),
         out_shape=fields,
-        in_specs=[pl.BlockSpec(memory_space=pltpu.VMEM)] * 4,
-        out_specs=[pl.BlockSpec(memory_space=pltpu.VMEM)] * 4,
-    )(*state)
+        in_specs=[whole] * 6,
+        out_specs=[whole] * 4,
+        scratch_shapes=[
+            pltpu.SMEM((2,), jnp.int32),
+            room(planes, 3, *box),
+            room(4, 3, planes, *plane),
+            dma((6,)),
+            dma((4,)),
+        ],
+        compiler_params=pltpu.CompilerParams(vmem_limit_bytes=60 * 1024 * 1024),
+    )(box_offset, mean, *state)
 
 
 def solution(mesh):

time: 42.5 us -> 40.5 us (0.953)
  Pallas kernels: 41.3 us -> 39.7 us
    pallas_call x1, Pallas kernels: 39 us -> 37.6 us  [on_device(): pl.pallas_call(functools.partial(kernel, n_slab, width, depth), out_shape...]
where the time goes in v3:
time: 40.5 us; the launch traced here: 40.4 us
  Pallas kernels  39.7 us (98%)
  between operations  0.64 us (2%)
    pallas_call x1, Pallas kernels, on_device(): pl.pallas_call(functools.partial(kernel, n_slab, width, depth), out_shape...  37.6 us
    pallas_call x1, Pallas kernels, on_device(): pl.pallas_call(functools.partial(hand_over, n_slab, width, depth), out_sh...  2.17 us

profile of v3, /device:TPU:99, one launch (start us, length us, event | category | flops | bytes accessed | tf_op | source)
XLA Modules:
  0.0 40.4 jit_solution(5730244937643369800)
XLA Ops:
  0.6 37.6 %shard_map.93 = (f32[1,3,3,24,384]{4,3,2,1,0:T(8,128)}, f32[1,3,3,24,384]{4,3,2,1,0:T(8,128)}, f32[1,3,3,24,384]{4,3,2,1,0:T(8,128)}, f32[1,3,3,24,384]{4,3,2,1,0:T(8,128)}, f32[3,3,8,128]{3,2,1,0:T(8,128)}) custom-call(s32[2]{0:T(128)} %off_in.3, f32[1,3,3,24,384]{4,3,2,1,0:T(8,128)} %e_in.1, f32[1,3,3,24,384]{4,3,2,1,0:T(8,128)} %h_in.1, ...), custom_call_target="tpu_custom_call" | custom-call | tf_op jit(solution)/shard_map/pallas_call | solution.py:858
  38.2 2.2 %shard_map.94 = (f32[1,3,3,24,384]{4,3,2,1,0:T(8,128)}, f32[1,3,3,24,384]{4,3,2,1,0:T(8,128)}, f32[1,3,3,24,384]{4,3,2,1,0:T(8,128)}, f32[1,3,3,24,384]{4,3,2,1,0:T(8,128)}) custom-call(s32[2]{0:T(128)} %off_in.3, f32[3,3,8,128]{3,2,1,0:T(8,128)} %get-tuple-element.9.mean_in, f32[1,3,3,24,384]{4,3,2,1,0:T(8,128)} %get-tuple-element.10.refs_0_, ...), custom_call_target="tpu_custom_call" | custom-call | tf_op jit(solution)/shard_map/pallas_call | solution.py:869

commit v4 on v3

--- a/solution.py
+++ b/solution.py
@@ -79,6 +79,72 @@
     return c_x, c_y, c_z
 
 
+def groups(few, many, many_dim):
+    shape = (few, many) if many_dim == 1 else (many, few)
+    return ones_where(iota(shape, many_dim) // 3 == iota(shape, 1 - many_dim))
+
+
+def ones_where(condition):
+    return jnp.where(condition, 1.0, 0.0).astype(jnp.bfloat16)
+
+
+def terms(value):
+    out = []
+    for _ in range(3):
+        out.append(value.astype(jnp.bfloat16))
+        value = value - out[-1].astype(jnp.float32)
+    return out
+
+
+def times(wide, matrix):
+    return sum(jnp.dot(t, matrix, preferred_element_type=jnp.float32) for t in terms(wide))
+
+
+def times_left(matrix, wide):
+    return sum(jnp.dot(matrix, t, preferred_element_type=jnp.float32) for t in terms(wide))
+
+
+def times_turned(matrix, wide):
+    return sum(
+        lax.dot_general(matrix, t, (((1,), (1,)), ((), ())), preferred_element_type=jnp.float32)
+        for t in terms(wide)
+    )
+
+
+def pack(sections):
+    box_y, box_z = sections[0].shape
+    tall = jnp.concatenate(sections, axis=0)
+    shape = (8, 3 * box_y)
+    row, column = iota(shape, 0), iota(shape, 1)
+    ends = ones_where((row < 6) & (column == (row // 2) * box_y + (row % 2) * (box_y - 1)))
+    shape = (8, box_z)
+    row, column = iota(shape, 0), iota(shape, 1)
+    sides = ones_where(((row == 6) & (column == 0)) | ((row == 7) & (column == box_z - 1)))
+    padded = jnp.concatenate([tall, jnp.zeros((box_z - 3 * box_y, box_z), jnp.float32)], axis=0)
+    return times_left(ends, tall) + times_turned(sides, padded)
+
+
+def unpack(packs, width, depth):
+    box_y, box_z = width // 3, depth // 3
+    tall = jnp.concatenate(packs, axis=0)
+    wide = times(tall, groups(box_z, depth, 1))
+    shape = (3 * width, box_z)
+    spread = times_turned(ones_where(iota(shape, 1) == iota(shape, 0) // 3), tall)
+    row, column = iota((width, depth), 0), iota((width, depth), 1)
+    planes = []
+    for j in range(len(packs)):
+        plane = []
+        for c in range(3):
+            at = 8 * j + 2 * c
+            side = spread[c * width : (c + 1) * width]
+            value = jnp.where(column == 0, side[:, 8 * j + 6 : 8 * j + 7], 0.0)
+            value = jnp.where(column == depth - 1, side[:, 8 * j + 7 : 8 * j + 8], value)
+            value = jnp.where(row == 0, wide[at : at + 1], value)
+            plane.append(jnp.where(row == width - 1, wide[at + 1 : at + 2], value))
+        planes.append(plane)
+    return planes
+
+
 def kernel(
     n_slab, width, depth,
     off_in, e_in, h_in, p_in, j_in, m_in,
@@ -87,10 +153,12 @@
     AE, AH, AQ, AJ, A1, BE, BH, partial,
     h_send, h_recv, b_send, b_recv,
     sec_send, sec_recv, table_send, table_recv, near_send, near_recv,
-    up_prev, up_last, mean_send, mean_recv, f_send, f_recv,
+    U, GA, DH, DJ, DQ, DE, mean_send, mean_recv, f_send, f_recv,
+    pack_send, pack_recv, kp_send, kp_recv, rim_send, rim_recv, D, d_send, d_recv,
     off_sem, load_sem, out_sem, m_sem,
     hs_sem, hr_sem, bs_sem, br_sem, ss_sem, sr_sem, ts_sem, tr_sem, ns_sem, nr_sem,
     ms_sem, mr_sem, fs_sem, fr_sem,
+    ps_sem, pr_sem, ks_sem, kr_sem, es_sem, er_sem, ds_sem, dr_sem,
 ):
     slab = lax.axis_index("slab")
     level = lax.axis_index("grid")
@@ -102,9 +170,16 @@
     has_right = slab < n_slab - 1
     partner_slab = first_slab + slab // 3
     partner_plane = slab % 3
-    borrows = partner_plane == 0
+    outer = (slab == 0) | (slab == n_slab - 1)
+    borrows = outer & (partner_plane == 0)
+    seam = jnp.where(partner_plane == 0, 1, jnp.where(partner_plane == 1, 0, 2))
+    has_seam = slab + seam - 1 < n_slab
+    near_fines = [3 * (slab - first_slab) + k for k in range(-1, PLANES + 2)]
+    listens = [(f >= 0) & (f < n_slab) for f in near_fines]
+    listens[0] = listens[0] & (near_fines[1] < n_slab)
     fine_at = [3 * (slab - first_slab) + p for p in range(PLANES + 1)]
     in_box = [(f >= 0) & (f < n_slab) for f in fine_at]
+    full_at = [(f == 0) | (f == n_slab - 1) for f in fine_at]
 
     fields = ((e_in, E, e_out), (h_in, H, h_out), (p_in, Q, p_out), (j_in, J, j_out))
     loads = [
@@ -124,7 +199,8 @@
         return sum(c.astype(jnp.int32) for c in conditions)
 
     greet(is_fine, {"grid": 0, "slab": partner_slab})
-    greet(is_fine & borrows, {"grid": 0, "slab": partner_slab - 1})
+    greet(is_fine & (partner_plane < 2), {"grid": 0, "slab": partner_slab - 1})
+    greet(is_fine & (partner_plane == 2) & has_right, {"grid": 0, "slab": partner_slab + 1})
     greet(has_left, {"slab": slab - 1})
     greet(has_right, {"slab": slab + 1})
 
@@ -182,6 +258,28 @@
 
     def f_copy(side):
         return remote(f_send, f_recv.at[side], fs_sem.at[side], fr_sem.at[side], right if side == 0 else left)
+
+    def pack_copy(index, p, k):
+        return remote(
+            pack_send.at[index, p], pack_recv.at[index, 2 - k], ps_sem.at[index, p, k], pr_sem.at[index, 2 - k],
+            {"grid": 1, "slab": fine_at[p] + k - 1},
+        )
+
+    def kp_copy(k):
+        return remote(kp_send, kp_recv, ks_sem.at[k], kr_sem, {"grid": 1, "slab": fine_at[0] + k - 1})
+
+    def rim_copy(index, k):
+        return remote(
+            rim_send.at[index], rim_recv.at[index], es_sem.at[index, k], er_sem.at[index],
+            {"grid": 1, "slab": fine_at[PLANES] + k - 1},
+        )
+
+    def d_copy(side):
+        return remote(d_send, d_recv.at[side], ds_sem.at[side], dr_sem.at[side], right if side == 0 else left)
+
+    def reaches(p, k):
+        target = fine_at[p] + k - 1
+        return in_box[p] & (target >= 0) & (target < n_slab)
 
     def go(condition, *copies):
         @pl.when(condition)
@@ -254,7 +352,11 @@
             scale = is_there if k == 3 else 1.0
             CR[k] = pick(near, [row[k] for row in values]) * scale
         CR[5] = pick(far, [row[3] for row in values]) * is_there
-        CL[...] = pick(m_left[...], [row[3] for row in values]) * has_left.astype(jnp.float32)
+        before = m_left[...]
+        CL[...] = pick(before, [row[3] for row in values]) * has_left.astype(jnp.float32)
+        gains = [1.0 - row[4] * row[2] for row in values]
+        for q, material in enumerate((before, M[0], M[1], M[2], near, far)):
+            GA[q] = pick(material, gains)
 
     def prepare():
         @pl.when(jnp.logical_not(has_left))
@@ -305,24 +407,6 @@
             & (slab >= 1) & (slab <= n_slab - 2)
         )
 
-        def groups(few, many, many_dim):
-            shape = (few, many) if many_dim == 1 else (many, few)
-            same = iota(shape, many_dim) // 3 == iota(shape, 1 - many_dim)
-            return jnp.where(same, 1.0, 0.0).astype(jnp.bfloat16)
-
-        def times(wide, matrix):
-            return sum(jnp.dot(t, matrix, preferred_element_type=jnp.float32) for t in terms(wide))
-
-        def times_left(matrix, wide):
-            return sum(jnp.dot(matrix, t, preferred_element_type=jnp.float32) for t in terms(wide))
-
-        def terms(value):
-            out = []
-            for _ in range(3):
-                out.append(value.astype(jnp.bfloat16))
-                value = value - out[-1].astype(jnp.float32)
-            return out
-
         def upsampled(section):
             section = section.reshape(3 * box_y, box_z)
             wide = times(section, groups(box_z, depth, 1))
@@ -334,9 +418,10 @@
             both = times(rows, groups(box_z, depth, 0))
             return (both * jnp.float32(1.0 / 27.0)).reshape(3, box_y, box_z)
 
-        def boundary(sub):
+        def boundary(b, sub, j=1):
             weight = jnp.float32((sub + 1) / 3.0)
-            return [up_prev[c] + weight * (up_last[c] - up_prev[c]) for c in range(3)]
+            before, after = U.at[b % 2, j], U.at[(b + 1) % 2, j]
+            return [before[c] + weight * (after[c] - before[c]) for c in range(3)]
 
         def inject(ref, index, p, values):
             for c in range(3):
@@ -352,17 +437,28 @@
         wait_loads((0, 0), (1, 0), (2, 0), (3, 0), (1, 2))
         prepare()
 
-        @pl.when(jnp.logical_not(borrows))
+        @pl.when(outer & jnp.logical_not(borrows))
         def _():
             near_recv[...] = jnp.zeros_like(near_recv)
+
+        @pl.when(jnp.logical_not(has_seam))
+        def _():
+            kp_recv[...] = jnp.zeros_like(kp_recv)
+            rim_recv[...] = jnp.zeros_like(rim_recv)
 
         @pl.when(jnp.logical_not(has_left))
         def _():
             f_recv[0] = jnp.zeros_like(f_recv[0])
+            d_recv[0] = jnp.zeros_like(d_recv[0])
+            for index in range(STEPS):
+                pack_recv[index, 0] = jnp.zeros_like(pack_recv[index, 0])
 
         @pl.when(jnp.logical_not(has_right))
         def _():
             f_recv[1] = jnp.zeros_like(f_recv[1])
+            d_recv[1] = jnp.zeros_like(d_recv[1])
+            for index in range(STEPS):
+                pack_recv[index, 2] = jnp.zeros_like(pack_recv[index, 2])
 
         pl.semaphore_wait(barrier, count(has_left, has_right))
         tell_right(0, H[2, 1], H[2, 2])
@@ -371,16 +467,85 @@
         go(has_right, m_to_right)
         wait_loads(*[(k, p) for k in range(4) for p in (1, 2) if (k, p) != (1, 2)])
 
-        def latest(index):
-            heard(True, section_copy(index, 0))
-            heard(borrows, near_copy(index))
-            k_c = table_recv[3]
-            base = sec_recv[index]
-            return (
-                base[0],
-                base[1] + k_c * near_recv[index, 1],
-                base[2] - k_c * near_recv[index, 0],
-            )
+        def fill(slot, packs, section):
+            for j, plane in enumerate(unpack(packs, width, depth)):
+                for c in range(3):
+                    U[slot, j, c] = plane[c]
+
+            @pl.when(outer)
+            def _():
+                whole = upsampled(section())
+                for c in range(3):
+                    U[slot, 1, c] = whole[c]
+
+        def rim_values(b):
+            heard(True, pack_copy(b, 0, 1))
+            heard(has_left, pack_copy(b, 0, 2))
+            heard(has_right, pack_copy(b, 0, 0))
+            heard(has_seam, rim_copy(b, 0))
+            heard(outer, section_copy(b, 0))
+            heard(borrows, near_copy(b))
+
+            @pl.when(b == 0)
+            def _():
+                heard(has_seam, kp_copy(0))
+                heard(True, table_copy(0))
+                fill(0, [pack_recv[0, j, 1] for j in range(3)], lambda: table_recv[0:3])
+
+            seamed = kp_recv[...] * rim_recv[b]
+            packs = [pack_recv[b, j, 0] + seamed * (seam == j).astype(jnp.float32) for j in range(3)]
+
+            def section(extra=None):
+                k_c = table_recv[3]
+                base = sec_recv[b]
+                parts = [
+                    base[0], base[1] + k_c * near_recv[b, 1], base[2] - k_c * near_recv[b, 0],
+                ]
+                if extra is not None:
+                    parts = [part + extra[c] for c, part in enumerate(parts)]
+                return jnp.stack(parts)
+
+            @pl.when(b < STEPS - 1)
+            def _():
+                fill((b + 1) % 2, packs, section)
+
+            @pl.when(b == STEPS - 1)
+            def _():
+                heard(has_left, d_copy(0))
+                heard(has_right, d_copy(1))
+                extras = (d_recv[0], d_send[...], d_recv[1])
+                fill((b + 1) % 2, [p + e for p, e in zip(packs, extras)], lambda: section(D))
+
+            first = [boundary(b, 0, 0)]
+            second = [None]
+            for p in range(PLANES):
+                first.append([jnp.where(rims[p], v, 0.0) for v in boundary(b, 0)])
+                second.append([jnp.where(rims[p], v, 0.0) for v in boundary(b, 1)])
+            first += [boundary(b, 0, 2)] * 2
+            second.append(boundary(b, 1, 2))
+            d_e = [[GA[q] * v for v in first[q]] for q in range(6)]
+            d_h = []
+            for q in range(5):
+                curl = curl_e(d_e[q], (d_e[q + 1][1], d_e[q + 1][2]))
+                d_h.append([-COURANT * u for u in curl])
+            there = has_left.astype(jnp.float32)
+            d_h[0] = [there * u for u in d_h[0]]
+            for p in range(PLANES):
+                put(DH, (p,), d_h[p + 1])
+            for p in (1, 2):
+                d_j = [CO[2, p] * v for v in first[p + 1]]
+                put(DJ, (p,), d_j)
+                put(DQ, (p,), [step * v for v in d_j])
+            for q, at in ((1, 0), (4, 1)):
+                a_j, a_p, a_e, k_c, k_j = [CO[k, 0] for k in range(5)] if at == 0 else [CR[k] for k in range(5)]
+                curl = curl_h(d_h[q], (d_h[q - 1][1], d_h[q - 1][2]))
+                for c in range(3):
+                    early = a_e * first[q][c]
+                    late = (a_j + step * a_p) * early + a_e * second[q][c]
+                    DE[at, c] = second[q][c] - k_j * late + k_c * curl[c]
+                    if at == 0:
+                        DJ[0, c] = late
+                        DQ[0, c] = step * (early + late)
 
         def feedback_response():
             heard(has_left, f_copy(0))
@@ -406,27 +571,10 @@
             curl = curl_e(get(AE), (E[1, 1], E[1, 2]))
             put(AH, (), [H[0, c] - COURANT * curl[c] for c in range(3)])
 
-            @pl.when(b == 0)
-            def _():
-                heard(True, table_copy(0))
-                up_last[...] = upsampled(table_recv[0:3])
-
-            up_prev[...] = up_last[...]
-            arrived = latest(b)
-
-            @pl.when(b < STEPS - 1)
-            def _():
-                up_last[...] = upsampled(jnp.stack(arrived))
-
-            @pl.when(b == STEPS - 1)
-            def _():
-                extra = feedback_response()
-                up_last[...] = upsampled(jnp.stack([a + e for a, e in zip(arrived, extra)]))
-
-            values = boundary(0)
-            inject(AE, (), 0, values)
-            inject(E, (1,), 1, values)
-            inject(E, (2,), 2, values)
+            nothing = [jnp.zeros((width, depth), jnp.float32)] * 3
+            inject(AE, (), 0, nothing)
+            inject(E, (1,), 1, nothing)
+            inject(E, (2,), 2, nothing)
             a_j, a_p, a_e, k_c, k_j = (CO[k, 0] for k in range(5))
             for c in range(3):
                 current = a_j * J[0, c] + a_p * Q[0, c] + a_e * AE[c]
@@ -450,8 +598,7 @@
             put(A1, (), e_1)
             curl = curl_e(get(AE), (A1[1], A1[2]))
             put(AH, (), [AH[c] - COURANT * curl[c] for c in range(3)])
-            values = boundary(1)
-            inject(AE, (), 0, values)
+            inject(AE, (), 0, nothing)
             for c in range(3):
                 current = a_j * AJ[c] + a_p * AQ[c] + a_e * AE[c]
                 AJ[c] = current
@@ -464,6 +611,19 @@
             @pl.when(b == 0)
             def _():
                 learn_neighbours(step)
+
+            @pl.when(b == 1)
+            def _():
+                extra = feedback_response()
+                for c in range(3):
+                    D[c] = extra[c]
+                d_send[...] = pack(extra)
+                go(has_right, d_copy(0))
+                go(has_left, d_copy(1))
+
+            @pl.when(b > 0)
+            def _():
+                rim_values(b)
 
             def face(coefficients, k_near, k_back, there, h_own, e_own, hear):
                 a_j, a_p, a_e, k_c, k_j = coefficients
@@ -538,14 +698,27 @@
             put(E, (1,), [A1[0], A1[1] + near[0], A1[2] + near[1]])
 
             magnetic_whole(1, true)
-            values = boundary(1)
+
+            @pl.when(b == 0)
+            def _():
+                rim_values(b)
+
+            next_y = next_y + DE[1, 1]
+            next_z = next_z + DE[1, 2]
+            values = boundary(b, 1)
+            for c in range(3):
+                for p in range(PLANES):
+                    H[p, c] = H[p, c] + DH[p, c]
+                    J[p, c] = J[p, c] + DJ[p, c]
+                    Q[p, c] = Q[p, c] + DQ[p, c]
+                AE[c] = AE[c] + DE[0, c]
             for p in (1, 2):
                 inject(E, (p,), p, values)
                 oscillate(p, step, true)
             electric_whole(2, true)
             electric_whole(1, true)
             magnetic_whole(1, true)
-            values = boundary(2)
+            values = boundary(b, 2)
             put(H, (2,), magnetic(2, true))
             near_y, near_z = E[1, 1], E[1, 2]
             for p in (1, 2):
@@ -601,8 +774,8 @@
         for slot in range(STEPS * SUBS):
             sent(has_right, h_copy(slot))
             sent(has_left, b_copy(slot))
-        sent(has_right, f_copy(0))
-        sent(has_left, f_copy(1))
+        sent(has_right, f_copy(0), d_copy(0))
+        sent(has_left, f_copy(1), d_copy(1))
         for index in range(STEPS):
             mean_copy(index).wait_send()
         written()
@@ -645,10 +818,23 @@
             for c in range(2):
                 near_send[index, c] = cut(state[1][2, 1 + c])
 
+        def get_section(index, p):
+            return [sec_send[index, p, c] for c in range(3)]
+
+        def take_rim(index):
+            zero = jnp.zeros((box_y, box_z), jnp.float32)
+            rim_send[index] = pack([zero, near_send[index, 1], -near_send[index, 0]])
+
         def send(index):
             for p in range(PLANES):
-                go(in_box[p], section_copy(index, p))
-            go(in_box[PLANES], near_copy(index))
+                for k in (1, 0, 2):
+                    go(reaches(p, k), pack_copy(index, p, k))
+                if p == 0:
+                    for k in range(3):
+                        go(reaches(PLANES, k), rim_copy(index, k))
+            for p in range(PLANES):
+                go(in_box[p] & full_at[p], section_copy(index, p))
+            go(in_box[PLANES] & full_at[PLANES], near_copy(index))
 
         def first_half(state, slot_h, slot_b):
             e, h, _, _ = state
@@ -690,13 +876,20 @@
         electric_whole(1, true)
         for p in (1, 2):
             take(0, p, get(E, p))
+        for p in range(PLANES):
+            pack_send[0, p, 0] = pack(get_section(0, p))
+            pack_send[0, p, 1] = pack([table_send[p, c] for c in range(3)])
+        kp_send[...] = pack([jnp.zeros((box_y, box_z), jnp.float32)] + [table_send[0, 3]] * 2)
+        take_rim(0)
         prepare()
-        pl.semaphore_wait(barrier, count(has_left, has_right, *in_box))
-        for p in range(PLANES):
-            go(in_box[p], table_copy(p), section_copy(0, p))
-        go(in_box[PLANES], near_copy(0))
+        pl.semaphore_wait(barrier, count(has_left, has_right, *listens))
+        for k in range(3):
+            go(reaches(0, k), kp_copy(k))
+        send(0)
         go(has_right, h_copy(0), m_to_right)
         go(has_left, b_copy(0), m_to_left)
+        for p in range(PLANES):
+            go(in_box[p], table_copy(p))
 
         magnetic_whole(1, true)
         learn_neighbours(step)
@@ -729,6 +922,10 @@
         electric_whole(1, guess)
         for p in (1, 2):
             take(1, p, get(TE, p))
+        take_rim(1)
+        for p in range(PLANES):
+            pack_send[1, p, 0] = pack(get_section(1, p))
+            pack_send[1, p, 1] = jnp.zeros((8, box_z), jnp.float32)
         send(1)
         heard(has_left, h_copy(1))
         k_c = CO[3, 0]
@@ -743,6 +940,9 @@
             oscillate(p, step, guess)
             back = None if p == 0 else (TH[p - 1, 1], TH[p - 1, 2])
             take(2, p, electric(p, guess, back))
+            pack_send[2, p, 0] = pack(get_section(2, p))
+            pack_send[2, p, 1] = jnp.zeros((8, box_z), jnp.float32)
+        take_rim(2)
         send(2)
 
         place(0)
@@ -766,8 +966,14 @@
         for slot in range(4):
             sent(has_left, b_copy(slot))
         for p in range(PLANES):
-            sent(in_box[p], table_copy(p), *[section_copy(index, p) for index in range(STEPS)])
-        sent(in_box[PLANES], *[near_copy(index) for index in range(STEPS)])
+            sent(in_box[p], table_copy(p))
+            sent(in_box[p] & full_at[p], *[section_copy(index, p) for index in range(STEPS)])
+            for k in range(3):
+                sent(reaches(p, k), *[pack_copy(index, p, k) for index in range(STEPS)])
+        for k in range(3):
+            sent(reaches(0, k), kp_copy(k))
+            sent(reaches(PLANES, k), *[rim_copy(index, k) for index in range(STEPS)])
+        sent(in_box[PLANES] & full_at[PLANES], *[near_copy(index) for index in range(STEPS)])
         written()
         for p in range(PLANES):
             heard(in_box[p], mean_arrival(STEPS - 1, p))
@@ -842,17 +1048,32 @@
         room(5, *box),
         room(STEPS, 2, *box),
         room(STEPS, 2, *box),
-        triple,
-        triple,
+        room(2, 3, 3, *plane),
+        room(6, *plane),
+        state,
+        state,
+        state,
+        room(2, 3, *plane),
         room(STEPS, 3, *box),
         room(STEPS - 1, planes, 3, *box),
         room(3, *box),
         room(2, 3, *box),
+        room(STEPS, planes, 2, 8, box[1]),
+        room(STEPS, 3, 2, 8, box[1]),
+        room(8, box[1]),
+        room(8, box[1]),
+        room(STEPS, 8, box[1]),
+        room(STEPS, 8, box[1]),
+        room(3, *box),
+        room(8, box[1]),
+        room(2, 8, box[1]),
     ]
     scratch += [dma, dma((5, planes)), dma((4, planes)), dma((4,))]
     scratch += [dma((slots,))] * 4
     scratch += [dma((STEPS, planes)), dma((STEPS,)), dma((planes,)), dma, dma((STEPS,)), dma((STEPS,))]
     scratch += [dma((STEPS,)), dma((STEPS, planes)), dma((2,)), dma((2,))]
+    scratch += [dma((STEPS, planes, 3)), dma((STEPS, 3)), dma((3,)), dma, dma((STEPS, 3)), dma((STEPS,))]
+    scratch += [dma((2,)), dma((2,))]
     whole = pl.BlockSpec(memory_space=pl.ANY)
     fields = [jax.ShapeDtypeStruct(efield.shape, f32)] * 4
     state = pl.pallas_call(

time: 40.5 us -> 39.9 us (0.985)
  Pallas kernels: 39.7 us -> 39.1 us
    pallas_call x1, Pallas kernels: 37.6 us -> 37 us  [on_device(): pl.pallas_call(functools.partial(kernel, n_slab, width, depth), out_shape...]
where the time goes in v4:
time: 39.9 us; the launch traced here: 39.8 us
  Pallas kernels  39.1 us (98%)
  between operations  0.64 us (2%)
    pallas_call x1, Pallas kernels, on_device(): pl.pallas_call(functools.partial(kernel, n_slab, width, depth), out_shape...  37 us
    pallas_call x1, Pallas kernels, on_device(): pl.pallas_call(functools.partial(hand_over, n_slab, width, depth), out_sh...  2.17 us

profile of v4, /device:TPU:99, one launch (start us, length us, event | category | flops | bytes accessed | tf_op | source)
XLA Modules:
  0.0 39.8 jit_solution(7502463571757097405)
XLA Ops:
  0.6 37.0 %shard_map.93 = (f32[1,3,3,24,384]{4,3,2,1,0:T(8,128)}, f32[1,3,3,24,384]{4,3,2,1,0:T(8,128)}, f32[1,3,3,24,384]{4,3,2,1,0:T(8,128)}, f32[1,3,3,24,384]{4,3,2,1,0:T(8,128)}, f32[3,3,8,128]{3,2,1,0:T(8,128)}) custom-call(s32[2]{0:T(128)} %off_in.3, f32[1,3,3,24,384]{4,3,2,1,0:T(8,128)} %e_in.1, f32[1,3,3,24,384]{4,3,2,1,0:T(8,128)} %h_in.1, ...), custom_call_target="tpu_custom_call" | custom-call | tf_op jit(solution)/shard_map/pallas_call | solution.py:1079
  37.6 2.2 %shard_map.94 = (f32[1,3,3,24,384]{4,3,2,1,0:T(8,128)}, f32[1,3,3,24,384]{4,3,2,1,0:T(8,128)}, f32[1,3,3,24,384]{4,3,2,1,0:T(8,128)}, f32[1,3,3,24,384]{4,3,2,1,0:T(8,128)}) custom-call(s32[2]{0:T(128)} %off_in.3, f32[3,3,8,128]{3,2,1,0:T(8,128)} %get-tuple-element.9.mean_in, f32[1,3,3,24,384]{4,3,2,1,0:T(8,128)} %get-tuple-element.10.refs_0_, ...), custom_call_target="tpu_custom_call" | custom-call | tf_op jit(solution)/shard_map/pallas_call | solution.py:1090

commit v5 on v4

--- a/solution.py
+++ b/solution.py
@@ -97,48 +97,61 @@
 
 
 def times(wide, matrix):
-    return sum(jnp.dot(t, matrix, preferred_element_type=jnp.float32) for t in terms(wide))
+    rows = wide.shape[0]
+    parts = jnp.dot(jnp.concatenate(terms(wide), axis=0), matrix, preferred_element_type=jnp.float32)
+    return parts[:rows] + parts[rows : 2 * rows] + parts[2 * rows :]
 
 
 def times_left(matrix, wide):
-    return sum(jnp.dot(matrix, t, preferred_element_type=jnp.float32) for t in terms(wide))
-
-
-def times_turned(matrix, wide):
-    return sum(
-        lax.dot_general(matrix, t, (((1,), (1,)), ((), ())), preferred_element_type=jnp.float32)
-        for t in terms(wide)
-    )
-
-
-def pack(sections):
-    box_y, box_z = sections[0].shape
-    tall = jnp.concatenate(sections, axis=0)
-    shape = (8, 3 * box_y)
-    row, column = iota(shape, 0), iota(shape, 1)
-    ends = ones_where((row < 6) & (column == (row // 2) * box_y + (row % 2) * (box_y - 1)))
-    shape = (8, box_z)
-    row, column = iota(shape, 0), iota(shape, 1)
-    sides = ones_where(((row == 6) & (column == 0)) | ((row == 7) & (column == box_z - 1)))
-    padded = jnp.concatenate([tall, jnp.zeros((box_z - 3 * box_y, box_z), jnp.float32)], axis=0)
-    return times_left(ends, tall) + times_turned(sides, padded)
-
-
-def unpack(packs, width, depth):
+    tall = jnp.concatenate(terms(wide), axis=0)
+    return jnp.dot(jnp.concatenate([matrix] * 3, axis=1), tall, preferred_element_type=jnp.float32)
+
+
+def ends(values, first):
+    shape = next(v for v in values if v is not None).shape
+    row, lane = iota(shape, 0), iota(shape, 1)
+    flat = (8, shape[1])
+    flat_row = iota(flat, 0)
+    rows, columns = jnp.zeros(flat, jnp.float32), jnp.zeros(shape, jnp.float32)
+    for c, value in enumerate(values):
+        if value is not None:
+            for side, at, column in ((0, first, 0), (1, first + 7, shape[1] - 1)):
+                if isinstance(first, int):
+                    taken = value[at : at + 1]
+                else:
+                    taken = jnp.sum(jnp.where(row == at, value, 0.0), axis=0, keepdims=True)
+                rows = jnp.where(flat_row == 2 * c + side, taken, rows)
+                columns = jnp.where(lane == 2 * c + side, value[:, column : column + 1], columns)
+    return rows, columns
+
+
+def fold(rows, columns):
+    columns = jnp.where(iota(columns.shape, 1) < 8, columns, 0.0)
+    line = jnp.sum(pltpu.roll(columns, 0, 1, stride=8, stride_axis=0), axis=0, keepdims=True)
+    return jnp.where(iota(rows.shape, 0) == 6, line, rows)
+
+
+def unfold(packed):
+    line = jnp.broadcast_to(packed[6:7], packed.shape)
+    out, row = line, iota(packed.shape, 0)
+    for y in range(1, 8):
+        out = jnp.where(row == y, pltpu.roll(line, packed.shape[1] - 8 * y, 1), out)
+    return out
+
+
+def unpack(rows, columns, width, depth):
     box_y, box_z = width // 3, depth // 3
-    tall = jnp.concatenate(packs, axis=0)
-    wide = times(tall, groups(box_z, depth, 1))
-    shape = (3 * width, box_z)
-    spread = times_turned(ones_where(iota(shape, 1) == iota(shape, 0) // 3), tall)
+    wide = times(jnp.concatenate(rows, axis=0), groups(box_z, depth, 1))
+    spread = times_left(groups(3 * box_y, 3 * width, 0), jnp.concatenate(columns, axis=0))
     row, column = iota((width, depth), 0), iota((width, depth), 1)
     planes = []
-    for j in range(len(packs)):
+    for j in range(3):
         plane = []
         for c in range(3):
-            at = 8 * j + 2 * c
-            side = spread[c * width : (c + 1) * width]
-            value = jnp.where(column == 0, side[:, 8 * j + 6 : 8 * j + 7], 0.0)
-            value = jnp.where(column == depth - 1, side[:, 8 * j + 7 : 8 * j + 8], value)
+            at, k = 8 * j + 2 * c, 2 * c
+            side = spread[j * width : (j + 1) * width]
+            value = jnp.where(column == 0, side[:, k : k + 1], 0.0)
+            value = jnp.where(column == depth - 1, side[:, k + 1 : k + 2], value)
             value = jnp.where(row == 0, wide[at : at + 1], value)
             plane.append(jnp.where(row == width - 1, wide[at + 1 : at + 2], value))
         planes.append(plane)
@@ -154,11 +167,11 @@
     h_send, h_recv, b_send, b_recv,
     sec_send, sec_recv, table_send, table_recv, near_send, near_recv,
     U, GA, DH, DJ, DQ, DE, mean_send, mean_recv, f_send, f_recv,
-    pack_send, pack_recv, kp_send, kp_recv, rim_send, rim_recv, D, d_send, d_recv,
+    pack_send, pack_recv, rim_send, rim_recv, D, d_send, d_recv,
     off_sem, load_sem, out_sem, m_sem,
     hs_sem, hr_sem, bs_sem, br_sem, ss_sem, sr_sem, ts_sem, tr_sem, ns_sem, nr_sem,
     ms_sem, mr_sem, fs_sem, fr_sem,
-    ps_sem, pr_sem, ks_sem, kr_sem, es_sem, er_sem, ds_sem, dr_sem,
+    ps_sem, pr_sem, es_sem, er_sem, ds_sem, dr_sem,
 ):
     slab = lax.axis_index("slab")
     level = lax.axis_index("grid")
@@ -204,6 +217,8 @@
     greet(has_left, {"slab": slab - 1})
     greet(has_right, {"slab": slab + 1})
 
+    load_off = pltpu.make_async_copy(off_in, off_ref, off_sem)
+    pl.when(is_coarse)(load_off.start)
     load_m.start()
     for p in range(PLANES):
         for k in range(4):
@@ -222,6 +237,7 @@
     def b_copy(slot):
         return remote(b_send.at[slot, 0:2], b_recv.at[slot], bs_sem.at[slot], br_sem.at[slot], left)
 
+    m_next = remote(m_in.at[0, 0:1], m_right.at[0:1], m_sem.at[0], m_sem.at[1], left)
     m_to_left = remote(m_in.at[0, 0:2], m_right, m_sem.at[0], m_sem.at[1], left)
     m_to_right = remote(m_in.at[0, 2], m_left, m_sem.at[2], m_sem.at[3], right)
 
@@ -234,6 +250,11 @@
     def table_copy(p):
         return remote(
             table_send.at[p], table_recv, ts_sem.at[p], tr_sem, {"grid": 1, "slab": fine_at[p]}
+        )
+
+    def gain_copy(p):
+        return remote(
+            table_send.at[p, 3:5], table_recv.at[3:5], ts_sem.at[p], tr_sem, {"grid": 1, "slab": fine_at[p]}
         )
 
     def near_copy(index):
@@ -260,13 +281,12 @@
         return remote(f_send, f_recv.at[side], fs_sem.at[side], fr_sem.at[side], right if side == 0 else left)
 
     def pack_copy(index, p, k):
+        size = 2 if isinstance(index, int) and index == 0 else 1
         return remote(
-            pack_send.at[index, p], pack_recv.at[index, 2 - k], ps_sem.at[index, p, k], pr_sem.at[index, 2 - k],
+            pack_send.at[index, p, 0:size], pack_recv.at[index, 2 - k, 0:size],
+            ps_sem.at[index, p, k], pr_sem.at[index, 2 - k],
             {"grid": 1, "slab": fine_at[p] + k - 1},
         )
-
-    def kp_copy(k):
-        return remote(kp_send, kp_recv, ks_sem.at[k], kr_sem, {"grid": 1, "slab": fine_at[0] + k - 1})
 
     def rim_copy(index, k):
         return remote(
@@ -443,7 +463,6 @@
 
         @pl.when(jnp.logical_not(has_seam))
         def _():
-            kp_recv[...] = jnp.zeros_like(kp_recv)
             rim_recv[...] = jnp.zeros_like(rim_recv)
 
         @pl.when(jnp.logical_not(has_left))
@@ -467,8 +486,8 @@
         go(has_right, m_to_right)
         wait_loads(*[(k, p) for k in range(4) for p in (1, 2) if (k, p) != (1, 2)])
 
-        def fill(slot, packs, section):
-            for j, plane in enumerate(unpack(packs, width, depth)):
+        def fill(slot, rows, columns, section):
+            for j, plane in enumerate(unpack(rows, columns, width, depth)):
                 for c in range(3):
                     U[slot, j, c] = plane[c]
 
@@ -479,21 +498,32 @@
                     U[slot, 1, c] = whole[c]
 
         def rim_values(b):
-            heard(True, pack_copy(b, 0, 1))
-            heard(has_left, pack_copy(b, 0, 2))
-            heard(has_right, pack_copy(b, 0, 0))
+            for index, now in ((0, b == 0), (b, b > 0)):
+                heard(now, pack_copy(index, 0, 1))
+                heard(now & has_left, pack_copy(index, 0, 2))
+                heard(now & has_right, pack_copy(index, 0, 0))
+
             heard(has_seam, rim_copy(b, 0))
             heard(outer, section_copy(b, 0))
             heard(borrows, near_copy(b))
 
             @pl.when(b == 0)
             def _():
-                heard(has_seam, kp_copy(0))
-                heard(True, table_copy(0))
-                fill(0, [pack_recv[0, j, 1] for j in range(3)], lambda: table_recv[0:3])
-
-            seamed = kp_recv[...] * rim_recv[b]
-            packs = [pack_recv[b, j, 0] + seamed * (seam == j).astype(jnp.float32) for j in range(3)]
+                heard(outer, table_copy(0))
+                before = [pack_recv[0, j, 1] for j in range(3)]
+                fill(0, before, [unfold(v) for v in before], lambda: table_recv[0:3])
+
+            near = rim_recv[b]
+            near_columns = unfold(near)
+            flat_row, lane = iota(near.shape, 0), iota(near.shape, 1)
+            rows, columns = [], []
+            for j in range(3):
+                here, origin = pack_recv[b, j, 0], pack_recv[0, j, 0]
+                sides = unfold(origin)
+                k_rows = jnp.where((flat_row == 2) | (flat_row == 4), origin[7:8], pack_recv[0, j, 1][7:8])
+                k_sides = jnp.where((lane == 2) | (lane == 4), sides[:, 6:7], sides[:, 7:8])
+                rows.append(here + jnp.where((flat_row >= 2) & (flat_row <= 5), k_rows * near, 0.0))
+                columns.append(unfold(here) + jnp.where((lane >= 2) & (lane <= 5), k_sides * near_columns, 0.0))
 
             def section(extra=None):
                 k_c = table_recv[3]
@@ -507,14 +537,17 @@
 
             @pl.when(b < STEPS - 1)
             def _():
-                fill((b + 1) % 2, packs, section)
+                fill((b + 1) % 2, rows, columns, section)
 
             @pl.when(b == STEPS - 1)
             def _():
                 heard(has_left, d_copy(0))
                 heard(has_right, d_copy(1))
                 extras = (d_recv[0], d_send[...], d_recv[1])
-                fill((b + 1) % 2, [p + e for p, e in zip(packs, extras)], lambda: section(D))
+                fill(
+                    (b + 1) % 2, [r + e for r, e in zip(rows, extras)],
+                    [k + unfold(e) for k, e in zip(columns, extras)], lambda: section(D),
+                )
 
             first = [boundary(b, 0, 0)]
             second = [None]
@@ -617,7 +650,7 @@
                 extra = feedback_response()
                 for c in range(3):
                     D[c] = extra[c]
-                d_send[...] = pack(extra)
+                d_send[...] = fold(*ends(extra, 0))
                 go(has_right, d_copy(0))
                 go(has_left, d_copy(1))
 
@@ -760,6 +793,7 @@
 
             @pl.when(b == 0)
             def _():
+                heard(jnp.logical_not(outer), gain_copy(0))
                 g = table_recv[4]
                 for c in range(3):
                     f_send[c] = jnp.where(f_cells, g * mean[c], 0.0)
@@ -783,8 +817,6 @@
     @pl.when(is_coarse)
     def _():
         step = STEP_COARSE
-        load_off = pltpu.make_async_copy(off_in, off_ref, off_sem)
-        load_off.start()
         load_off.wait()
         corner_y = off_ref[0]
         guess = (TE, TH, TQ, TJ)
@@ -810,20 +842,36 @@
                         kept = E[p, c, :, depth - box_z : depth]
                         E[p, c, :, depth - box_z : depth] = jnp.where(inside(p), placed, kept)
 
-        def take(index, p, values):
-            for c in range(3):
-                sec_send[index, p, c] = cut(values[c])
-
-        def take_near(index, state):
-            for c in range(2):
-                near_send[index, c] = cut(state[1][2, 1 + c])
-
-        def get_section(index, p):
-            return [sec_send[index, p, c] for c in range(3)]
-
-        def take_rim(index):
-            zero = jnp.zeros((box_y, box_z), jnp.float32)
-            rim_send[index] = pack([zero, near_send[index, 1], -near_send[index, 0]])
+        def box_part(value):
+            return value[:, depth - box_z : depth]
+
+        def with_row(rows, value, at):
+            taken = jnp.sum(jnp.where(iota(value.shape, 0) == at, value, 0.0), axis=0, keepdims=True)
+            return jnp.where(iota(rows.shape, 0) == 7, taken, rows)
+
+        def packed(rows, columns):
+            return fold(rows, pltpu.roll(columns, width - corner_y, 0)[:box_y])
+
+        def emit(index, p, values, scale=None):
+            rows, columns = ends([box_part(v) for v in values], corner_y)
+            if scale is not None:
+                lane = iota(columns.shape, 1)
+                columns = jnp.where(lane == 6, scale[:, 0:1], columns)
+                columns = jnp.where(lane == 7, scale[:, box_z - 1 : box_z], columns)
+                rows = with_row(rows, scale, corner_y)
+            pack_send[index, p, 0] = packed(rows, columns)
+
+            @pl.when(in_box[p] & full_at[p])
+            def _():
+                for c in range(3):
+                    sec_send[index, p, c] = cut(values[c])
+
+        def emit_near(index, y, z):
+            rim_send[index] = packed(*ends([None, box_part(z), -box_part(y)], corner_y))
+
+            @pl.when(in_box[PLANES] & full_at[PLANES])
+            def _():
+                near_send[index, 0], near_send[index, 1] = cut(y), cut(z)
 
         def send(index):
             for p in range(PLANES):
@@ -858,91 +906,98 @@
             )
             put(state[1], (2,), magnetic(2, state, ahead))
 
+        def guess_from(p):
+            for c in range(3):
+                value = E[p, c]
+                TE[p, c] = value
+                TE[p, c, :, depth - box_z : depth] = jnp.where(inside(p) & in_box[p], 0.0, box_part(value))
+                TQ[p, c] = Q[p, c]
+                TJ[p, c] = J[p, c]
+
         set_coefficients(step)
         wait_loads(*[(k, p) for k in range(4) for p in range(PLANES)])
-        for p in range(PLANES):
-            for c in range(3):
-                table_send[p, c] = cut(E[p, c])
-            table_send[p, 3] = cut(CO[3, p])
-            table_send[p, 4] = 1.0 - cut(CO[4, p]) * cut(CO[2, p])
         h_send[0, 0], h_send[0, 1] = H[2, 1], H[2, 2]
-        take_near(0, true)
-        for p in range(PLANES):
-            oscillate(p, step, true)
+        oscillate(0, step, true)
         start = electric(0, true)
         set_b(0, start)
-        take(0, 0, start)
-        electric_whole(2, true)
-        electric_whole(1, true)
-        for p in (1, 2):
-            take(0, p, get(E, p))
+        emit_near(0, H[2, 1], H[2, 2])
+        scale = box_part(CO[3, 0])
         for p in range(PLANES):
-            pack_send[0, p, 0] = pack(get_section(0, p))
-            pack_send[0, p, 1] = pack([table_send[p, c] for c in range(3)])
-        kp_send[...] = pack([jnp.zeros((box_y, box_z), jnp.float32)] + [table_send[0, 3]] * 2)
-        take_rim(0)
+            rows, columns = ends([box_part(E[p, c]) for c in range(3)], corner_y)
+            if p == 0:
+                rows = with_row(rows, scale, corner_y + box_y - 1)
+            pack_send[0, p, 1] = packed(rows, columns)
+
+            @pl.when(in_box[p] & full_at[p])
+            def _(p=p):
+                for c in range(3):
+                    table_send[p, c] = cut(E[p, c])
+
+        emit(0, 0, start, scale)
+        for p in (2, 1):
+            oscillate(p, step, true)
+            electric_whole(p, true)
+            emit(0, p, get(E, p))
         prepare()
         pl.semaphore_wait(barrier, count(has_left, has_right, *listens))
-        for k in range(3):
-            go(reaches(0, k), kp_copy(k))
         send(0)
-        go(has_right, h_copy(0), m_to_right)
-        go(has_left, b_copy(0), m_to_left)
+        go(has_right, h_copy(0))
+        go(has_left, b_copy(0), m_next)
         for p in range(PLANES):
-            go(in_box[p], table_copy(p))
+
+            @pl.when(in_box[p])
+            def _(p=p):
+                table_send[p, 3] = cut(CO[3, p])
+                table_send[p, 4] = 1.0 - cut(CO[4, p]) * cut(CO[2, p])
+                go(full_at[p], table_copy(p))
+                go(jnp.logical_not(full_at[p]), gain_copy(p))
 
         magnetic_whole(1, true)
-        learn_neighbours(step)
+        for p in (1, 2):
+            guess_from(p)
+            oscillate(p, step, guess)
+        for c in range(3):
+            TH[1, c] = H[1, c]
         heard(has_left, h_copy(0))
         k_c = CO[3, 0]
         E[0, 0] = start[0]
         E[0, 1] = b_send[0, 0] + k_c * h_recv[0, 1]
         E[0, 2] = b_send[0, 1] - k_c * h_recv[0, 0]
         magnetic_whole(0, true)
-        second_half(true, 0, 0)
-        tell_right(1, H[2, 1], H[2, 2])
-
-        take_near(1, true)
-        for p in range(PLANES):
-            for c in range(3):
-                value = E[p, c]
-                TE[p, c] = value
-                kept = value[:, depth - box_z : depth]
-                TE[p, c, :, depth - box_z : depth] = jnp.where(inside(p) & in_box[p], 0.0, kept)
-                TH[p, c] = H[p, c]
-                TQ[p, c] = Q[p, c]
-                TJ[p, c] = J[p, c]
+        guess_from(0)
+        for c in range(3):
+            TH[0, c] = H[0, c]
         oscillate(0, step, guess)
         start = electric(0, guess)
         tell_left(1, start)
-        take(1, 0, start)
+        emit(1, 0, start)
+        electric_whole(1, guess)
+        emit(1, 1, get(TE, 1))
+        heard(has_right, m_next)
+        sent(has_left, m_next)
+        CR[3] = pick(m_right[0], [row[3] for row in tables(step)]) * has_right.astype(jnp.float32)
+        second_half(true, 0, 0)
+        tell_right(1, H[2, 1], H[2, 2])
+        emit_near(1, H[2, 1], H[2, 2])
+        for c in range(3):
+            TH[2, c] = H[2, c]
+        electric_whole(2, guess)
+        emit(1, 2, get(TE, 2))
+        send(1)
+        magnetic_whole(1, guess)
         for p in (1, 2):
             oscillate(p, step, guess)
-        electric_whole(2, guess)
-        electric_whole(1, guess)
-        for p in (1, 2):
-            take(1, p, get(TE, p))
-        take_rim(1)
-        for p in range(PLANES):
-            pack_send[1, p, 0] = pack(get_section(1, p))
-            pack_send[1, p, 1] = jnp.zeros((8, box_z), jnp.float32)
-        send(1)
         heard(has_left, h_copy(1))
-        k_c = CO[3, 0]
         TE[0, 0] = b_send[1, 2]
         TE[0, 1] = b_send[1, 0] + k_c * h_recv[1, 1]
         TE[0, 2] = b_send[1, 1] - k_c * h_recv[1, 0]
-        magnetic_whole(1, guess)
         magnetic_whole(0, guess)
+        oscillate(0, step, guess)
+        emit(2, 0, electric(0, guess))
+        emit(2, 1, electric(1, guess, (TH[0, 1], TH[0, 2])))
         second_half(guess, 1, 1)
-        take_near(2, guess)
-        for p in range(PLANES):
-            oscillate(p, step, guess)
-            back = None if p == 0 else (TH[p - 1, 1], TH[p - 1, 2])
-            take(2, p, electric(p, guess, back))
-            pack_send[2, p, 0] = pack(get_section(2, p))
-            pack_send[2, p, 1] = jnp.zeros((8, box_z), jnp.float32)
-        take_rim(2)
+        emit_near(2, TH[2, 1], TH[2, 2])
+        emit(2, 2, electric(2, guess, (TH[1, 1], TH[1, 2])))
         send(2)
 
         place(0)
@@ -966,12 +1021,12 @@
         for slot in range(4):
             sent(has_left, b_copy(slot))
         for p in range(PLANES):
-            sent(in_box[p], table_copy(p))
+            sent(in_box[p] & full_at[p], table_copy(p))
+            sent(in_box[p] & jnp.logical_not(full_at[p]), gain_copy(p))
             sent(in_box[p] & full_at[p], *[section_copy(index, p) for index in range(STEPS)])
             for k in range(3):
                 sent(reaches(p, k), *[pack_copy(index, p, k) for index in range(STEPS)])
         for k in range(3):
-            sent(reaches(0, k), kp_copy(k))
             sent(reaches(PLANES, k), *[rim_copy(index, k) for index in range(STEPS)])
         sent(in_box[PLANES] & full_at[PLANES], *[near_copy(index) for index in range(STEPS)])
         written()
@@ -1060,8 +1115,6 @@
         room(2, 3, *box),
         room(STEPS, planes, 2, 8, box[1]),
         room(STEPS, 3, 2, 8, box[1]),
-        room(8, box[1]),
-        room(8, box[1]),
         room(STEPS, 8, box[1]),
         room(STEPS, 8, box[1]),
         room(3, *box),
@@ -1072,7 +1125,7 @@
     scratch += [dma((slots,))] * 4
     scratch += [dma((STEPS, planes)), dma((STEPS,)), dma((planes,)), dma, dma((STEPS,)), dma((STEPS,))]
     scratch += [dma((STEPS,)), dma((STEPS, planes)), dma((2,)), dma((2,))]
-    scratch += [dma((STEPS, planes, 3)), dma((STEPS, 3)), dma((3,)), dma, dma((STEPS, 3)), dma((STEPS,))]
+    scratch += [dma((STEPS, planes, 3)), dma((STEPS, 3)), dma((STEPS, 3)), dma((STEPS,))]
     scratch += [dma((2,)), dma((2,))]
     whole = pl.BlockSpec(memory_space=pl.ANY)
     fields = [jax.ShapeDtypeStruct(efield.shape, f32)] * 4

time: 39.9 us -> 38.4 us (0.962)
  Pallas kernels: 39.1 us -> 37.6 us
    pallas_call x1, Pallas kernels: 37 us -> 35.4 us  [on_device(): pl.pallas_call(functools.partial(kernel, n_slab, width, depth), out_shape...]
where the time goes in v5:
time: 38.4 us; the launch traced here: 38.2 us
  Pallas kernels  37.6 us (98%)
  between operations  0.64 us (2%)
    pallas_call x1, Pallas kernels, on_device(): pl.pallas_call(functools.partial(kernel, n_slab, width, depth), out_shape...  35.4 us
    pallas_call x1, Pallas kernels, on_device(): pl.pallas_call(functools.partial(hand_over, n_slab, width, depth), out_sh...  2.17 us

profile of v5, /device:TPU:99, one launch (start us, length us, event | category | flops | bytes accessed | tf_op | source)
XLA Modules:
  0.0 38.2 jit_solution(18237943656788183415)
XLA Ops:
  0.6 35.4 %shard_map.93 = (f32[1,3,3,24,384]{4,3,2,1,0:T(8,128)}, f32[1,3,3,24,384]{4,3,2,1,0:T(8,128)}, f32[1,3,3,24,384]{4,3,2,1,0:T(8,128)}, f32[1,3,3,24,384]{4,3,2,1,0:T(8,128)}, f32[3,3,8,128]{3,2,1,0:T(8,128)}) custom-call(s32[2]{0:T(128)} %off_in.3, f32[1,3,3,24,384]{4,3,2,1,0:T(8,128)} %e_in.1, f32[1,3,3,24,384]{4,3,2,1,0:T(8,128)} %h_in.1, ...), custom_call_target="tpu_custom_call" | custom-call | tf_op jit(solution)/shard_map/pallas_call | solution.py:1132
  36.0 2.2 %shard_map.94 = (f32[1,3,3,24,384]{4,3,2,1,0:T(8,128)}, f32[1,3,3,24,384]{4,3,2,1,0:T(8,128)}, f32[1,3,3,24,384]{4,3,2,1,0:T(8,128)}, f32[1,3,3,24,384]{4,3,2,1,0:T(8,128)}) custom-call(s32[2]{0:T(128)} %off_in.3, f32[3,3,8,128]{3,2,1,0:T(8,128)} %get-tuple-element.9.mean_in, f32[1,3,3,24,384]{4,3,2,1,0:T(8,128)} %get-tuple-element.10.refs_0_, ...), custom_call_target="tpu_custom_call" | custom-call | tf_op jit(solution)/shard_map/pallas_call | solution.py:1143

commit v6 on v5

--- a/solution.py
+++ b/solution.py
@@ -940,9 +940,9 @@
             emit(0, p, get(E, p))
         prepare()
         pl.semaphore_wait(barrier, count(has_left, has_right, *listens))
-        send(0)
         go(has_right, h_copy(0))
         go(has_left, b_copy(0), m_next)
+        send(0)
         for p in range(PLANES):
 
             @pl.when(in_box[p])

time: 38.4 us -> 37.7 us (0.982)
  the two profiles are of different devices: /device:TPU:99 before, /device:TPU:2 now
where the time goes in v6:
time: 37.7 us; the launch traced here: 37.5 us
  Pallas kernels  36.9 us (98%)
  between operations  0.64 us (2%)
    pallas_call x1, Pallas kernels, on_device(): pl.pallas_call(functools.partial(kernel, n_slab, width, depth), out_shape...  34.7 us
    pallas_call x1, Pallas kernels, on_device(): pl.pallas_call(functools.partial(hand_over, n_slab, width, depth), out_sh...  2.17 us

profile of v6, /device:TPU:2, one launch (start us, length us, event | category | flops | bytes accessed | tf_op | source)
XLA Modules:
  0.0 37.5 jit_solution(1396917135523299418)
XLA Ops:
  0.6 34.7 %shard_map.93 = (f32[1,3,3,24,384]{4,3,2,1,0:T(8,128)}, f32[1,3,3,24,384]{4,3,2,1,0:T(8,128)}, f32[1,3,3,24,384]{4,3,2,1,0:T(8,128)}, f32[1,3,3,24,384]{4,3,2,1,0:T(8,128)}, f32[3,3,8,128]{3,2,1,0:T(8,128)}) custom-call(s32[2]{0:T(128)} %off_in.3, f32[1,3,3,24,384]{4,3,2,1,0:T(8,128)} %e_in.1, f32[1,3,3,24,384]{4,3,2,1,0:T(8,128)} %h_in.1, ...), custom_call_target="tpu_custom_call" | custom-call | tf_op jit(solution)/shard_map/pallas_call | solution.py:1132
  35.4 2.2 %shard_map.94 = (f32[1,3,3,24,384]{4,3,2,1,0:T(8,128)}, f32[1,3,3,24,384]{4,3,2,1,0:T(8,128)}, f32[1,3,3,24,384]{4,3,2,1,0:T(8,128)}, f32[1,3,3,24,384]{4,3,2,1,0:T(8,128)}) custom-call(s32[2]{0:T(128)} %off_in.3, f32[3,3,8,128]{3,2,1,0:T(8,128)} %get-tuple-element.9.mean_in, f32[1,3,3,24,384]{4,3,2,1,0:T(8,128)} %get-tuple-element.10.refs_0_, ...), custom_call_target="tpu_custom_call" | custom-call | tf_op jit(solution)/shard_map/pallas_call | solution.py:1143

commit v7 on v6

--- a/solution.py
+++ b/solution.py
@@ -970,14 +970,14 @@
         oscillate(0, step, guess)
         start = electric(0, guess)
         tell_left(1, start)
-        emit(1, 0, start)
-        electric_whole(1, guess)
-        emit(1, 1, get(TE, 1))
         heard(has_right, m_next)
         sent(has_left, m_next)
         CR[3] = pick(m_right[0], [row[3] for row in tables(step)]) * has_right.astype(jnp.float32)
         second_half(true, 0, 0)
         tell_right(1, H[2, 1], H[2, 2])
+        emit(1, 0, start)
+        electric_whole(1, guess)
+        emit(1, 1, get(TE, 1))
         emit_near(1, H[2, 1], H[2, 2])
         for c in range(3):
             TH[2, c] = H[2, c]

time: 37.7 us -> 37.5 us (level)
  no operation moved by 1% of the time
where the time goes in v7:
time: 37.5 us; the launch traced here: 37.3 us
  Pallas kernels  36.7 us (98%)
  between operations  0.64 us (2%)
    pallas_call x1, Pallas kernels, on_device(): pl.pallas_call(functools.partial(kernel, n_slab, width, depth), out_shape...  34.5 us
    pallas_call x1, Pallas kernels, on_device(): pl.pallas_call(functools.partial(hand_over, n_slab, width, depth), out_sh...  2.17 us

profile of v7, /device:TPU:2, one launch (start us, length us, event | category | flops | bytes accessed | tf_op | source)
XLA Modules:
  0.0 37.3 jit_solution(16346260762515578261)
XLA Ops:
  0.6 34.5 %shard_map.93 = (f32[1,3,3,24,384]{4,3,2,1,0:T(8,128)}, f32[1,3,3,24,384]{4,3,2,1,0:T(8,128)}, f32[1,3,3,24,384]{4,3,2,1,0:T(8,128)}, f32[1,3,3,24,384]{4,3,2,1,0:T(8,128)}, f32[3,3,8,128]{3,2,1,0:T(8,128)}) custom-call(s32[2]{0:T(128)} %off_in.3, f32[1,3,3,24,384]{4,3,2,1,0:T(8,128)} %e_in.1, f32[1,3,3,24,384]{4,3,2,1,0:T(8,128)} %h_in.1, ...), custom_call_target="tpu_custom_call" | custom-call | tf_op jit(solution)/shard_map/pallas_call | solution.py:1132
  35.2 2.2 %shard_map.94 = (f32[1,3,3,24,384]{4,3,2,1,0:T(8,128)}, f32[1,3,3,24,384]{4,3,2,1,0:T(8,128)}, f32[1,3,3,24,384]{4,3,2,1,0:T(8,128)}, f32[1,3,3,24,384]{4,3,2,1,0:T(8,128)}) custom-call(s32[2]{0:T(128)} %off_in.3, f32[3,3,8,128]{3,2,1,0:T(8,128)} %get-tuple-element.9.mean_in, f32[1,3,3,24,384]{4,3,2,1,0:T(8,128)} %get-tuple-element.10.refs_0_, ...), custom_call_target="tpu_custom_call" | custom-call | tf_op jit(solution)/shard_map/pallas_call | solution.py:1143
